TPU v7x, 1024 devices: a whole 8x8x8 slice. The times are simulated.
1024 devices in a mesh: dp: 8 (over y), ctx: 4 (over x_lo, core), tp: 32 (over z, x_hi).
Axes of the slice: x: 8 (x_hi: 4, x_lo: 2; x = x_hi * 2 + x_lo), y: 8, z: 8, core: 2. Of those that a mesh axis runs over, the one named last changes fastest.
Arguments:
- tokens: bfloat16 [4, 64, 4096], P('ctx', 'dp'), may hold values from -6 to 6
- cotangent: bfloat16 [4, 64, 4096], P('ctx', 'dp'), may hold values from -6 to 6
- routes: int32 [4, 64, 8], P('ctx'), may hold values from 0 to 127, all different within a row; in each aligned block of 64 rows (0 to 63, 64 to 127, ..., all dimensions but the last counted through in order) at most 6 rows name the same one
- probs: bfloat16 [4, 64, 8], P('ctx'), may hold values from 0.029907227 to 0.3984375
- w_gate: bfloat16 [128, 4096, 1024], P(('ctx', 'tp'), None, 'dp'), may hold values from -0.09375 to 0.09375
- w_up: bfloat16 [128, 4096, 1024], P(('ctx', 'tp'), None, 'dp'), may hold values from -0.09375 to 0.09375
- w_down: bfloat16 [128, 1024, 4096], P(('ctx', 'tp'), 'dp'), may hold values from -0.1875 to 0.1875
Outputs:
- mixed: bfloat16 [4, 64, 4096], P('ctx', 'tp', 'dp')
- input_grad: bfloat16 [4, 64, 4096], P('ctx', 'tp', 'dp')
Inputs may be any that keep to these rules, and one draw needn't show every extreme that they name: `routes`: in each column every expert is named by at most 6 of its 64 rows, and a token never names one expert twice.
All inputs are finite; a program needn't handle non-finite values.
Results may differ from a plain program's by a relative error of at most 0.023.
Values may be sent and summed in bfloat16 or wider, within the bound.
No kernel may reach another device: no remote copies, remote signals or barrier semaphores. Data moves between devices by JAX's collectives and lax.ppermute only.
A program may use at most 32 MiB of HBM per device.

v0:
```python
import jax
import jax.numpy as jnp
from jax import lax
from jax.sharding import PartitionSpec as P


def column_slots(route_ids, expert_count):
    matches = (route_ids[..., None] == jnp.arange(expert_count, dtype=jnp.int32)).astype(jnp.int32)
    per_row = jnp.sum(matches, axis=-2)
    before = jnp.cumsum(per_row, axis=-2) - per_row
    return jnp.sum(matches * before[..., None, :], axis=-1)


def gather_slots(selector, row_block):
    packed = lax.dot_general(
        selector, row_block, (((0,), (0,)), ((), ())), preferred_element_type=jnp.float32
    )
    return packed.astype(jnp.bfloat16)


def contract_last(left, right):
    return lax.dot_general(
        left, right, (((1,), (1,)), ((), ())), preferred_element_type=jnp.float32
    )


def body(tokens, cotangent, routes, probs, w_gate, w_up, w_down):
    dp_count = lax.axis_size("dp")
    ctx_count = lax.axis_size("ctx")
    tp_count = lax.axis_size("tp")
    route_ids = routes[0]
    weight = probs[0]
    column, top_count = route_ids.shape
    width = tokens.shape[2]
    expert_count = ctx_count * tp_count
    capacity = min(column, 3 * column * top_count // (2 * expert_count))
    slot_count = ctx_count * capacity
    slots = column_slots(route_ids, expert_count)
    owned_route = route_ids % tp_count == lax.axis_index("tp")
    position = route_ids // tp_count * capacity + slots
    matches = (position[:, :, None] == jnp.arange(slot_count, dtype=jnp.int32)) & owned_route[
        :, :, None
    ]
    chosen = jnp.any(matches, axis=1).astype(jnp.bfloat16)
    scaling = jnp.sum(
        jnp.where(matches, weight[:, :, None].astype(jnp.float32), 0.0), axis=1
    ).astype(jnp.bfloat16)
    slice_width = width // dp_count
    part_x, part_dy = (
        lax.all_to_all(tokens[0], "dp", split_axis=1, concat_axis=0, tiled=True),
        lax.all_to_all(cotangent[0], "dp", split_axis=1, concat_axis=0, tiled=True),
    )
    packed_x = gather_slots(chosen, part_x).reshape(ctx_count, capacity, slice_width)
    packed_dy = gather_slots(scaling, part_dy).reshape(ctx_count, capacity, slice_width)
    moved_x, moved_dy = (
        lax.all_to_all(packed_x, "ctx", split_axis=0, concat_axis=0, tiled=True),
        lax.all_to_all(packed_dy, "ctx", split_axis=0, concat_axis=0, tiled=True),
    )
    sent_x, sent_dy = (
        lax.all_gather(moved_x, "dp", axis=2, tiled=True),
        lax.all_gather(moved_dy, "dp", axis=2, tiled=True),
    )
    expert_x = sent_x.reshape(slot_count, width)
    expert_dy = sent_dy.reshape(slot_count, width)
    gate_weight = w_gate[0]
    up_weight = w_up[0]
    down_weight = w_down[0]
    gate_pre = jnp.dot(expert_x, gate_weight, preferred_element_type=jnp.float32)
    up_pre = jnp.dot(expert_x, up_weight, preferred_element_type=jnp.float32)
    sigmoid_gate = jax.nn.sigmoid(gate_pre)
    hidden = (gate_pre * sigmoid_gate * up_pre).astype(jnp.bfloat16)
    out_term = jnp.dot(hidden, down_weight, preferred_element_type=jnp.float32)
    hidden_grad = contract_last(expert_dy, down_weight)
    gate_grad = (
        hidden_grad * up_pre * sigmoid_gate * (1.0 + gate_pre * (1.0 - sigmoid_gate))
    ).astype(jnp.bfloat16)
    up_grad = (hidden_grad * gate_pre * sigmoid_gate).astype(jnp.bfloat16)
    both_grads = jnp.concatenate((gate_grad, up_grad), axis=1)
    both_weights = jnp.concatenate((gate_weight, up_weight), axis=1)
    input_term = contract_last(both_grads, both_weights)
    tok_rows = column // tp_count
    summed_out, summed_grad = (
        lax.psum_scatter(
            out_term.astype(jnp.bfloat16), "dp", scatter_dimension=1, tiled=True
        ).astype(jnp.float32),
        lax.psum_scatter(
            input_term.astype(jnp.bfloat16), "dp", scatter_dimension=1, tiled=True
        ).astype(jnp.float32),
    )
    back_out, back_grad = (
        lax.all_to_all(
            summed_out.reshape(ctx_count, capacity, slice_width).astype(jnp.bfloat16),
            "ctx",
            split_axis=0,
            concat_axis=0,
            tiled=True,
        ).astype(jnp.float32),
        lax.all_to_all(
            summed_grad.reshape(ctx_count, capacity, slice_width).astype(jnp.bfloat16),
            "ctx",
            split_axis=0,
            concat_axis=0,
            tiled=True,
        ).astype(jnp.float32),
    )
    mixed_block = jnp.dot(
        scaling.astype(jnp.float32),
        back_out.reshape(slot_count, slice_width),
        precision=lax.Precision.HIGHEST,
        preferred_element_type=jnp.float32,
    )
    grad_block = jnp.dot(
        chosen.astype(jnp.float32),
        back_grad.reshape(slot_count, slice_width),
        precision=lax.Precision.HIGHEST,
        preferred_element_type=jnp.float32,
    )
    mixed, input_grad = (
        lax.psum_scatter(
            mixed_block.astype(jnp.bfloat16), "tp", scatter_dimension=0, tiled=True
        ).astype(jnp.float32),
        lax.psum_scatter(
            grad_block.astype(jnp.bfloat16), "tp", scatter_dimension=0, tiled=True
        ).astype(jnp.float32),
    )
    mixed = mixed.astype(jnp.bfloat16).reshape(1, tok_rows, slice_width)
    input_grad = input_grad.astype(jnp.bfloat16).reshape(1, tok_rows, slice_width)
    return (mixed, input_grad)


def solution(mesh):
    placed = (
        P("ctx", "dp", None),
        P("ctx", "dp", None),
        P("ctx", None, None),
        P("ctx", None, None),
        P(("ctx", "tp"), None, "dp"),
        P(("ctx", "tp"), None, "dp"),
        P(("ctx", "tp"), "dp", None),
    )
    return jax.shard_map(
        body,
        mesh=mesh,
        in_specs=placed,
        out_specs=(P("ctx", "tp", "dp"), P("ctx", "tp", "dp")),
        check_vma=False,
    )
```

profile of v0, /device:TPU:32, one launch (start us, length us, event | category | flops | bytes accessed | tf_op | source)
XLA Modules:
  0.0 513.2 jit_solution(11698927209900439684)
XLA Ops:
  7.2 16.2 %all-to-all-start = ((bf16[8,8,512]{2,0,1:T(8,128)(2,1)}), bf16[8,8,512]{2,0,1:T(8,128)(2,1)S(1)}, u32[]{:S(2)}, u32[]{:S(2)}) async-start(bf16[8,8,512]{2,0,1:T(8,128)(2,1)} %bitcast.47), calls=%async_computation | async-start | bytes 131072 | tf_op jit(solution)/shard_map/all_to_all | solution.py:50
  24.4 1.2 select_reduce_fusion
  27.8 1.5 all-to-all-done
  29.3 5.9 %all-to-all-start.3 = ((bf16[8,8,512]{2,0,1:T(8,128)(2,1)}), bf16[8,8,512]{2,0,1:T(8,128)(2,1)S(1)}, u32[]{:S(2)}, u32[]{:S(2)}) async-start(bf16[8,8,512]{2,0,1:T(8,128)(2,1)} %bitcast.48), calls=%async_computation.4 | async-start | bytes 131072 | tf_op jit(solution)/shard_map/all_to_all | solution.py:51
  36.0 5.2 %all-to-all-done.3 = bf16[8,8,512]{2,0,1:T(8,128)(2,1)S(1)} async-done(((bf16[8,8,512]{2,0,1:T(8,128)(2,1)}), bf16[8,8,512]{2,0,1:T(8,128)(2,1)S(1)}, u32[]{:S(2)}, u32[]{:S(2)}) %all-to-all-start.3) | async-done | bytes 65568 | tf_op jit(solution)/shard_map/all_to_all | solution.py:51
  41.1 3.3 all-to-all-start.1
  45.2 3.2 all-to-all-done.1
  48.3 3.3 all-to-all-start.4
  51.6 24.6 %all_gather.6 = bf16[4,6,4096]{2,1,0:T(8,128)(2,1)S(1)} all-gather(bf16[4,6,512]{2,1,0:T(8,128)(2,1)S(1)} %all-to-all-done.1), channel_id=1, replica_groups=mesh['dp'=8,'ctx'=4,'tp'=32] {'dp'}, dimensions={2}, use_global_device_ids=true | all-gather | bytes 221184 | tf_op jit(solution)/shard_map/all_gather | solution.py:60
  76.3 24.8 %all_gather.7 = bf16[4,6,4096]{2,1,0:T(8,128)(2,1)S(1)} all-gather(bf16[4,6,512]{2,1,0:T(8,128)(2,1)S(1)} %all-to-all-done.4), channel_id=1, replica_groups=mesh['dp'=8,'ctx'=4,'tp'=32] {'dp'}, dimensions={2}, use_global_device_ids=true | all-gather | bytes 221184 | tf_op jit(solution)/shard_map/all_gather | solution.py:61
  102.8 1.3 convolution_convert_fusion
  104.2 0.9 convolution_convert_fusion.1
  105.1 40.4 %reduce-scatter.5.cloned.1.call-done = bf16[24,512]{1,0:T(8,128)(2,1)} async-done(((bf16[24,4096]{1,0:T(8,128)(2,1)}), bf16[24,512]{1,0:T(8,128)(2,1)}) %reduce-scatter.5.cloned.1.call-update) | async-done | bytes 24592 | tf_op jit(solution)/shard_map/reduce_scatter | solution.py:86
  145.5 1.4 convert_element_type.76
  146.9 3.3 all-to-all-start.5
  150.1 40.5 %reduce-scatter.3.cloned.1.call-done = bf16[24,512]{1,0:T(8,128)(2,1)} async-done(((bf16[24,4096]{1,0:T(8,128)(2,1)}), bf16[24,512]{1,0:T(8,128)(2,1)}) %reduce-scatter.3.cloned.1.call-update) | async-done | bytes 24592 | tf_op jit(solution)/shard_map/reduce_scatter | solution.py:83
  190.6 1.4 convert_element_type.70
  191.9 3.3 all-to-all-start.2
  195.3 0.8 convolution_convert_fusion.2
  196.1 3.0 all-to-all-done.2
  199.1 0.8 convolution_convert_fusion.3
  200.0 1.3 dynamic-slice
  201.9 303.4 %all-reduce.5.cloned.1.call-done = (bf16[64,512]{1,0:T(8,128)(2,1)}, bf16[64,512]{1,0:T(8,128)(2,1)}) async-done(((bf16[64,512]{1,0:T(8,128)(2,1)}, bf16[64,512]{1,0:T(8,128)(2,1)}), (bf16[64,512]{1,0:T(8,128)(2,1)}, bf16[64,512]{1,0:T(8,128)(2,1)})) %all-reduce.5.cloned.1.call-update) | async-done | bytes 131088
  505.3 1.3 dynamic-slice_bitcast_fusion
  (35 shorter events, 6.6 us)
Async XLA Ops:
  7.2 94.4 %copy-start = (bf16[1,128,4096]{2,1,0:T(8,128)(2,1)S(1)}, bf16[1,128,4096]{2,1,0:T(8,128)(2,1)}, u32[]{:S(2)}) copy-start(bf16[1,128,4096]{2,1,0:T(8,128)(2,1)} %param.13) | copy-start | bytes 3145732
  7.2 22.1 %all-to-all-start = ((bf16[8,8,512]{2,0,1:T(8,128)(2,1)}), bf16[8,8,512]{2,0,1:T(8,128)(2,1)S(1)}, u32[]{:S(2)}, u32[]{:S(2)}) async-start(bf16[8,8,512]{2,0,1:T(8,128)(2,1)} %bitcast.47), calls=%async_computation | async-start | bytes 131072 | tf_op jit(solution)/shard_map/all_to_all | solution.py:50
  27.8 73.4 %copy-start.2 = (bf16[1,4096,128]{2,1,0:T(8,128)(2,1)S(1)}, bf16[1,4096,128]{2,1,0:T(8,128)(2,1)}, u32[]{:S(2)}) copy-start(bf16[1,4096,128]{2,1,0:T(8,128)(2,1)} %param.12) | copy-start | bytes 3145732
  29.3 11.8 %all-to-all-start.3 = ((bf16[8,8,512]{2,0,1:T(8,128)(2,1)}), bf16[8,8,512]{2,0,1:T(8,128)(2,1)S(1)}, u32[]{:S(2)}, u32[]{:S(2)}) async-start(bf16[8,8,512]{2,0,1:T(8,128)(2,1)} %bitcast.48), calls=%async_computation.4 | async-start | bytes 131072 | tf_op jit(solution)/shard_map/all_to_all | solution.py:51
  41.1 7.2 %all-to-all-start.1 = ((bf16[4,6,512]{2,1,0:T(8,128)(2,1)}), bf16[4,6,512]{2,1,0:T(8,128)(2,1)S(1)}, u32[]{:S(2)}, u32[]{:S(2)}) async-start(bf16[4,6,512]{2,1,0:T(8,128)(2,1)} %reshape.113), calls=%async_computation.1 | async-start | bytes 65536 | tf_op jit(solution)/shard_map/all_to_all | solution.py:56
  48.3 28.0 %all-to-all-start.4 = ((bf16[4,6,512]{2,1,0:T(8,128)(2,1)}), bf16[4,6,512]{2,1,0:T(8,128)(2,1)S(1)}, u32[]{:S(2)}, u32[]{:S(2)}) async-start(bf16[4,6,512]{2,1,0:T(8,128)(2,1)} %reshape.117), calls=%async_computation.5 | async-start | bytes 65536 | tf_op jit(solution)/shard_map/all_to_all | solution.py:57
  51.6 93.9 %reduce-scatter.5.cloned.1.call-start = ((), (), s32[]{:S(2)}) async-start(), calls=%async_computation.9 | async-start | bytes 221184 | tf_op jit(solution)/shard_map/reduce_scatter | solution.py:86
  101.2 1.2 copy-start.1
  104.1 86.5 %reduce-scatter.3.cloned.1.call-start = ((), (), s32[]{:S(2)}) async-start(), calls=%async_computation.8 | async-start | bytes 221184 | tf_op jit(solution)/shard_map/reduce_scatter | solution.py:83
  146.9 45.1 %all-to-all-start.5 = ((bf16[4,6,512]{2,1,0:T(8,128)(2,1)}), bf16[4,6,512]{2,1,0:T(8,128)(2,1)S(1)}, u32[]{:S(2)}, u32[]{:S(2)}) async-start(bf16[4,6,512]{2,1,0:T(8,128)(2,1)} %convert_element_type.76), calls=%async_computation.7 | async-start | bytes 65536 | tf_op jit(solution)/shard_map/all_to_all | solution.py:98
  191.9 7.2 %all-to-all-start.2 = ((bf16[4,6,512]{2,1,0:T(8,128)(2,1)}), bf16[4,6,512]{2,1,0:T(8,128)(2,1)S(1)}, u32[]{:S(2)}, u32[]{:S(2)}) async-start(bf16[4,6,512]{2,1,0:T(8,128)(2,1)} %convert_element_type.70), calls=%async_computation.3 | async-start | bytes 65536 | tf_op jit(solution)/shard_map/all_to_all | solution.py:91
  195.2 310.1 %all-reduce.5.cloned.1.call-start = ((), (), s32[]{:S(2)}) async-start(), calls=%async_computation.10 | async-start | bytes 262144
Sparse Core Ops, SparseCore 0:
  104.2 41.2 reduce-scatter.4
  149.2 41.2 reduce-scatter.2
  200.1 305.1 all-reduce.4
where the time goes:
time: 514 us; the launch traced here: 513 us
  waiting for transfers between devices  397 us (77%)
  blocking collectives  49.4 us (10%)
  starting transfers between devices  35.2 us (7%)
  between operations  14.5 us (3%)
  local copies, waits for them, and re-layouts  8.08 us (2%)
  matrix products  5.17 us (1%)
    unnamed x4, waiting for transfers between devices  303 us
    reduce_scatter x1, waiting for transfers between devices, body(): lax.psum_scatter(out_term.astype(jnp.bfloat16), 'dp', scatter_dimension=1...  40.5 us
    reduce_scatter x1, waiting for transfers between devices, body(): lax.psum_scatter(input_term.astype(jnp.bfloat16), 'dp', scatter_dimension...  40.4 us
    all_gather x1, blocking collectives, body(): lax.all_gather(moved_dy, 'dp', axis=2, tiled=True)  24.8 us
    all_gather x1, blocking collectives, body(): lax.all_gather(moved_x, 'dp', axis=2, tiled=True)  24.6 us
    all_to_all x1, starting transfers between devices, body(): lax.all_to_all(tokens[0], 'dp', split_axis=1, concat_axis=0, tiled=True)  16.2 us
  transfers between devices with their start and end apart: 9, of which 7 were waited for; matrix products, arithmetic and copies ran while one was open for 2% of the time, Pallas kernels for 0%

commit v1 on v0

v1 whole, which is shorter than its diff:
```python
import jax
import jax.numpy as jnp
from jax import lax
from jax.sharding import PartitionSpec as P

BF16 = jnp.bfloat16
F32 = jnp.float32
ROWS = 8


def column_slots(route_ids, expert_count):
    matches = (route_ids[..., None] == jnp.arange(expert_count, dtype=jnp.int32)).astype(jnp.int32)
    per_row = jnp.sum(matches, axis=-2)
    before = jnp.cumsum(per_row, axis=-2) - per_row
    return jnp.sum(matches * before[..., None, :], axis=-1)


def contract_last(left, right):
    return lax.dot_general(
        left, right, (((1,), (1,)), ((), ())), preferred_element_type=F32
    )


def body(tokens, cotangent, routes, probs, w_gate, w_up, w_down):
    dp_count = lax.axis_size("dp")
    ctx_count = lax.axis_size("ctx")
    tp_count = lax.axis_size("tp")
    both_axes = ("ctx", "dp")
    pairs = ctx_count * dp_count
    route_ids = routes[0]
    weight = probs[0]
    column, _ = route_ids.shape
    own_rows, width = tokens.shape[1:]
    slice_width = width // dp_count
    expert_count = ctx_count * tp_count
    slot_rows = ctx_count * ROWS

    sent = jnp.concatenate((tokens[0], cotangent[0]), axis=0)
    parts = lax.all_to_all(sent, "dp", split_axis=1, concat_axis=0, tiled=True)

    slots = column_slots(route_ids, expert_count)
    owned_route = route_ids % tp_count == lax.axis_index("tp")
    position = route_ids // tp_count * ROWS + slots
    matches = (position[:, :, None] == jnp.arange(slot_rows, dtype=jnp.int32)) & owned_route[
        :, :, None
    ]
    chosen = jnp.any(matches, axis=1).astype(BF16)
    scaling = jnp.sum(
        jnp.where(matches, weight[:, :, None].astype(F32), 0.0), axis=1
    ).astype(BF16)
    kinds = jnp.stack((chosen, scaling)).reshape(2, dp_count, own_rows, ctx_count, ROWS)
    eye = jnp.eye(2, dtype=BF16)
    selector = (kinds.transpose(3, 0, 4, 1, 2)[:, :, :, :, None, :] * eye[None, :, None, None, :, None])
    selector = selector.reshape(ctx_count * 2 * ROWS, dp_count * 2 * own_rows)

    packed = jnp.dot(selector, parts, preferred_element_type=F32).astype(BF16)
    packed = jnp.broadcast_to(
        packed.reshape(ctx_count, 1, 2 * ROWS, slice_width),
        (ctx_count, dp_count, 2 * ROWS, slice_width),
    ).reshape(pairs, 2 * ROWS, slice_width)
    moved = lax.all_to_all(packed, both_axes, split_axis=0, concat_axis=0, tiled=True)
    moved = moved.reshape(ctx_count, dp_count, 2, ROWS, slice_width).transpose(2, 0, 3, 1, 4)
    expert_x, expert_dy = moved.reshape(2, slot_rows, width)

    gate_weight = w_gate[0]
    up_weight = w_up[0]
    down_weight = w_down[0]
    gate_pre = jnp.dot(expert_x, gate_weight, preferred_element_type=F32)
    up_pre = jnp.dot(expert_x, up_weight, preferred_element_type=F32)
    sigmoid_gate = jax.nn.sigmoid(gate_pre)
    hidden = (gate_pre * sigmoid_gate * up_pre).astype(BF16)
    out_term = jnp.dot(hidden, down_weight, preferred_element_type=F32)
    hidden_grad = contract_last(expert_dy, down_weight)
    gate_grad = (
        hidden_grad * up_pre * sigmoid_gate * (1.0 + gate_pre * (1.0 - sigmoid_gate))
    ).astype(BF16)
    up_grad = (hidden_grad * gate_pre * sigmoid_gate).astype(BF16)
    input_term = contract_last(gate_grad, gate_weight) + contract_last(up_grad, up_weight)

    terms = jnp.stack((out_term.astype(BF16), input_term.astype(BF16)))
    terms = terms.reshape(2, ctx_count, ROWS, dp_count, slice_width).transpose(1, 3, 0, 2, 4)
    back = lax.all_to_all(
        terms.reshape(pairs, 2 * ROWS, slice_width), both_axes, split_axis=0, concat_axis=0, tiled=True
    )
    back = jnp.sum(
        back.reshape(ctx_count, dp_count, 2, ROWS, slice_width).astype(F32), axis=1
    ).astype(BF16)
    mixed = jnp.dot(
        scaling, back[:, 0].reshape(slot_rows, slice_width), preferred_element_type=F32
    )
    grad = jnp.dot(
        chosen, back[:, 1].reshape(slot_rows, slice_width), preferred_element_type=F32
    )
    tok_rows = column // tp_count
    per_owner = jnp.stack(
        (
            mixed.astype(BF16).reshape(tp_count, tok_rows, slice_width),
            grad.astype(BF16).reshape(tp_count, tok_rows, slice_width),
        ),
        axis=1,
    ).reshape(tp_count, 2 * tok_rows, slice_width)
    got = lax.all_to_all(per_owner, "tp", split_axis=0, concat_axis=0, tiled=True)
    got = jnp.sum(got.astype(F32), axis=0).astype(BF16).reshape(2, 1, tok_rows, slice_width)
    return got[0], got[1]


def solution(mesh):
    placed = (
        P("ctx", "dp", None),
        P("ctx", "dp", None),
        P("ctx", None, None),
        P("ctx", None, None),
        P(("ctx", "tp"), None, "dp"),
        P(("ctx", "tp"), None, "dp"),
        P(("ctx", "tp"), "dp", None),
    )
    return jax.shard_map(
        body,
        mesh=mesh,
        in_specs=placed,
        out_specs=(P("ctx", "tp", "dp"), P("ctx", "tp", "dp")),
        check_vma=False,
    )
```

time: 514 us -> 99.4 us (0.19)
  the two profiles are of different devices: /device:TPU:32 before, /device:TPU:2 now
where the time goes in v1:
time: 99.4 us; the launch traced here: 98.9 us
  blocking collectives  75.2 us (76%)
  starting transfers between devices  7.56 us (8%)
  waiting for transfers between devices  5.08 us (5%)
  other arithmetic  3.85 us (4%)
  local copies, waits for them, and re-layouts  3.68 us (4%)
  matrix products  2.76 us (3%)
    all_to_all x1, blocking collectives, body(): lax.all_to_all(packed, both_axes, split_axis=0, concat_axis=0, tiled=True)  28.2 us
    all_to_all x1, blocking collectives, body(): lax.all_to_all(per_owner, 'tp', split_axis=0, concat_axis=0, tiled=True)  25.9 us
    all_to_all x1, blocking collectives, body(): lax.all_to_all(terms.reshape(pairs, 2 * ROWS, slice_width), both_axes, sp...  21.1 us
    all_to_all x1, starting transfers between devices, body(): parts = lax.all_to_all(sent, 'dp', split_axis=1, concat_axis=0, tiled=True)  7.56 us
    all_to_all x1, waiting for transfers between devices, body(): parts = lax.all_to_all(sent, 'dp', split_axis=1, concat_axis=0, tiled=True)  5.08 us
    unnamed x10, local copies, waits for them, and re-layouts  2.22 us
  transfers between devices with their start and end apart: 1, of which 1 were waited for; matrix products, arithmetic and copies ran while one was open for 3% of the time, Pallas kernels for 0%

profile of v1, /device:TPU:2, one launch (start us, length us, event | category | flops | bytes accessed | tf_op | source)
XLA Modules:
  0.0 98.9 jit_solution(3453858730249786860)
XLA Ops:
  0.6 1.6 %pad_maximum_fusion.1 = bf16[16,8,512]{2,0,1:T(8,128)(2,1)} fusion(bf16[8,8,512]{2,0,1:T(8,128)(2,1)} %bitcast.81, bf16[8,8,512]{2,0,1:T(8,128)(2,1)} %bitcast.82), kind=kLoop, calls=%fused_computation.21 | loop fusion | flops 262144 | bytes 262144 | tf_op jit(solution)/shard_map/concatenate | solution.py:38
  2.3 7.6 %all-to-all-start = ((bf16[16,8,512]{2,0,1:T(8,128)(2,1)}), bf16[16,8,512]{2,0,1:T(8,128)(2,1)S(1)}, u32[]{:S(2)}, u32[]{:S(2)}) async-start(bf16[16,8,512]{2,0,1:T(8,128)(2,1)} %pad_maximum_fusion.1), calls=%async_computation | async-start | bytes 262144 | tf_op jit(solution)/shard_map/all_to_all | solution.py:39
  9.8 0.7 copy-done.3
  10.6 0.1 convert_reduce_fusion
  10.8 1.2 %select_reduce_fusion = s32[64,8]{1,0:T(8,128)S(1)} fusion(s32[64,128]{1,0:T(8,128)S(1)} %sub.17, s32[64,8]{1,0:T(8,128)S(1)} %copy.42), kind=kLoop, calls=%fused_computation.17 | loop fusion | flops 196096 | bytes 36864 | tf_op jit(solution)/shard_map/reduce_sum | solution.py:15
  12.2 0.7 copy-done.4
  13.1 0.4 broadcast_multiply_fusion
  13.6 0.2 mul.72
  13.8 5.1 %all-to-all-done = bf16[16,8,512]{2,0,1:T(8,128)(2,1)S(1)} async-done(((bf16[16,8,512]{2,0,1:T(8,128)(2,1)}), bf16[16,8,512]{2,0,1:T(8,128)(2,1)S(1)}, u32[]{:S(2)}, u32[]{:S(2)}) %all-to-all-start) | async-done | bytes 131104 | tf_op jit(solution)/shard_map/all_to_all | solution.py:39
  18.9 0.1 convolution_convert_fusion.3
  19.1 28.2 %all_to_all.31 = bf16[32,16,512]{2,1,0:T(8,128)(2,1)S(1)} all-to-all(bf16[32,16,512]{2,1,0:T(8,128)(2,1)S(1)} %bitcast.73), channel_id=1, replica_groups=mesh['dp'=8,'ctx'=4,'tp'=32] {'ctx','dp'}, dimensions={0} | all-to-all | bytes 1048576 | tf_op jit(solution)/shard_map/all_to_all | solution.py:61
  47.4 0.3 fusion.9
  47.7 0.9 copy-done.1
  48.5 0.3 fusion.5
  48.9 0.4 fusion.1
  49.3 0.3 convolution_convert_fusion
  49.6 0.5 fusion.7
  50.0 0.5 fusion
  50.6 21.1 %all_to_all.32 = bf16[32,16,512]{2,1,0:T(8,128)(2,1)S(1)} all-to-all(bf16[32,16,512]{2,1,0:T(8,128)(2,1)S(1)} %bitcast.72), channel_id=1, replica_groups=mesh['dp'=8,'ctx'=4,'tp'=32] {'ctx','dp'}, dimensions={0} | all-to-all | bytes 1048576 | tf_op jit(solution)/shard_map/all_to_all | solution.py:82
  71.7 0.2 convolution_convert_fusion.2
  71.9 0.2 convolution_convert_fusion.1
  72.3 0.1 copy.49
  72.4 25.9 %all_to_all.33 = bf16[32,4,512]{2,1,0:T(4,128)(2,1)S(1)} all-to-all(bf16[32,4,512]{2,1,0:T(4,128)(2,1)S(1)} %copy.49), channel_id=1, replica_groups=mesh['dp'=8,'ctx'=4,'tp'=32] {'tp'}, dimensions={0} | all-to-all | bytes 262144 | tf_op jit(solution)/shard_map/all_to_all | solution.py:102
  98.4 0.6 slice_bitcast_fusion.4
  (30 shorter events, 1.0 us)
Async XLA Ops:
  0.6 48.2 %copy-start = (bf16[1,128,4096]{2,1,0:T(8,128)(2,1)S(1)}, bf16[1,128,4096]{2,1,0:T(8,128)(2,1)}, u32[]{:S(2)}) copy-start(bf16[1,128,4096]{2,1,0:T(8,128)(2,1)} %param.13) | copy-start | bytes 3145732
  2.3 16.7 %all-to-all-start = ((bf16[16,8,512]{2,0,1:T(8,128)(2,1)}), bf16[16,8,512]{2,0,1:T(8,128)(2,1)S(1)}, u32[]{:S(2)}, u32[]{:S(2)}) async-start(bf16[16,8,512]{2,0,1:T(8,128)(2,1)} %pad_maximum_fusion.1), calls=%async_computation | async-start | bytes 262144 | tf_op jit(solution)/shard_map/all_to_all | solution.py:39
  9.8 0.7 copy-start.3
  12.2 0.7 copy-start.4
  19.1 28.2 %copy-start.2 = (bf16[1,4096,128]{2,1,0:T(8,128)(2,1)S(1)}, bf16[1,4096,128]{2,1,0:T(8,128)(2,1)}, u32[]{:S(2)}) copy-start(bf16[1,4096,128]{2,1,0:T(8,128)(2,1)} %param.11) | copy-start | bytes 3145732
  47.3 1.2 %copy-start.1 = (bf16[1,4096,128]{2,1,0:T(8,128)(2,1)S(1)}, bf16[1,4096,128]{2,1,0:T(8,128)(2,1)}, u32[]{:S(2)}) copy-start(bf16[1,4096,128]{2,1,0:T(8,128)(2,1)} %param.12) | copy-start | bytes 3145732

commit v2 on v1

v2 whole, which is shorter than its diff:
```python
import jax
import jax.numpy as jnp
from jax import lax
from jax.experimental import pallas as pl
from jax.experimental.pallas import tpu as pltpu
from jax.sharding import Mesh, PartitionSpec as P

BF16 = jnp.bfloat16
F32 = jnp.float32
I32 = jnp.int32
DP = ("ya", "yb")
TP = ("za", "zb", "xh")
X_PARTS = 4
CAP = 6
ROWS = 8
CUTS = 4
LANES = 128


def sixth(v):
    return (v * 10923) >> 16


def iota(shape, dim):
    return lax.broadcasted_iota(I32, shape, dim)


def dot(left, right):
    return jnp.dot(left, right, preferred_element_type=F32)


def dot_t(left, right):
    return lax.dot_general(
        left, right, (((1,), (1,)), ((), ())), preferred_element_type=F32
    )


def params(mib):
    return pltpu.CompilerParams(vmem_limit_bytes=mib << 20)


def spread_kernel(at_ref, tok_ref, cot_ref, out_ref, sems):
    own = at_ref[1]
    block = out_ref.shape[3]
    copies = []
    for d in range(out_ref.shape[0]):
        for kind, ref in enumerate((tok_ref, cot_ref)):
            start = pl.multiple_of(((d % 2) * 2 + own) * block, block)
            copies.append(
                pltpu.make_async_copy(
                    ref.at[0, :, pl.ds(start, block)], out_ref.at[d, kind], sems.at[2 * d + kind]
                )
            )
    for copy in copies:
        copy.start()
    for copy in copies:
        copy.wait()


def selector_kernel(ctx_count, tp_count, at_ref, routes_ref, probs_ref, pack_ref, mix_ref):
    za, zb, xh = at_ref[0], at_ref[1], at_ref[2]
    top, column = routes_ref.shape
    columns = 2 * column
    experts = ctx_count * tp_count
    expert = iota((experts, columns), 0).astype(F32)
    named = jnp.zeros((experts, columns), F32)
    share = jnp.zeros((experts, columns), F32)

    def token(j):
        return ((j >> 4) << 3) + (j & 7)

    def kind_of(j):
        return (j >> 3) & 1

    shape = (column, columns)
    spread = (iota(shape, 0) == token(iota(shape, 1))).astype(F32).astype(BF16)
    routes = dot(routes_ref[...].astype(F32).astype(BF16), spread)
    probs = dot(probs_ref[...], spread)
    for k in range(top):
        hit = routes[k : k + 1, :] == expert
        named = jnp.where(hit, 1.0, named)
        share = jnp.where(hit, probs[k : k + 1, :], share)

    row, col = iota((columns, columns), 0), iota((columns, columns), 1)
    earlier = ((kind_of(row) == 0) & (token(row) < token(col))).astype(F32).astype(BF16)
    named = named.astype(BF16)
    before = dot(named, earlier)
    table = jnp.concatenate((named, share.astype(BF16), before.astype(BF16)), axis=1)

    def picked(expert_rows, slot_rows):
        wanted = (expert_rows == iota(expert_rows.shape, 1)).astype(F32).astype(BF16)
        got = dot(wanted, table)
        valid = (got[:, :columns] > 0.5) & (
            got[:, 2 * columns :] == slot_rows.astype(F32)
        )
        return valid, got[:, columns : 2 * columns]

    row = iota((ctx_count * 2 * CUTS * 2 * CAP, LANES), 0)
    outer = sixth(row)
    slot = row - CAP * outer
    kind = outer & 1
    cut = (outer >> 1) & 3
    far = outer >> 3
    owner = (far >> 1) * tp_count + (za * 2 + (far & 1)) * X_PARTS + xh
    valid, scale = picked(owner, slot)
    mine = valid & (kind == kind_of(iota(row.shape, 1)))
    value = jnp.where(mine, jnp.where(kind == 1, scale, 1.0), 0.0)
    for c in range(CUTS):
        pack_ref[:, c * LANES : (c + 1) * LANES] = jnp.where(cut == c, value, 0.0).astype(BF16)

    row = iota((ctx_count * CUTS * 2 * CAP, LANES), 0)
    outer = sixth(row)
    slot = row - CAP * outer
    kind = outer & 1
    owner = (outer >> 3) * tp_count + (za * 2 + zb) * X_PARTS + xh
    valid, scale = picked(owner, slot)
    value = jnp.where(valid, jnp.where(kind == 0, scale, 1.0), 0.0).astype(BF16)
    shape = (mix_ref.shape[0], LANES)
    row, col = iota(shape, 0), iota(shape, 1)
    wanted = (kind_of(col) == 0) & (token(col) == ((row >> 4) << 1) + (row & 1))
    full = dot_t(wanted.astype(F32).astype(BF16), value)
    row, col = iota(full.shape, 0), sixth(iota(full.shape, 1))
    same = (((row >> 1) & 1) == (col & 1)) & (((row >> 2) & 3) == ((col >> 1) & 3))
    mix_ref[...] = jnp.where(same, full, 0.0).astype(BF16)


def pack_kernel(pack_ref, got_ref, out_ref):
    sources, rows, block = got_ref.shape
    got = got_ref[...].reshape(sources * rows, block)
    part = block // CUTS
    stacked = jnp.concatenate([got[:, c * part : (c + 1) * part] for c in range(CUTS)], axis=0)
    packed = dot(pack_ref[...], stacked).astype(BF16)
    size = out_ref.shape[1]
    for to in range(out_ref.shape[0]):
        c, zb = to >> 2, to & 1
        first = (c * 2 + zb) * size
        out_ref[to] = packed[first : first + size]


def expert_kernel(ctx_count, got_ref, gate_ref, up_ref, down_ref, out_ref):
    _, size, part = got_ref.shape
    blocks = got_ref.shape[0] // ctx_count
    width, hidden_rows = gate_ref.shape
    slot_rows = ctx_count * ROWS
    arrived = jnp.concatenate(
        [
            jnp.concatenate([got_ref[c * blocks + q] for q in range(blocks)], axis=1)
            for c in range(ctx_count)
        ],
        axis=0,
    )

    def source(v):
        slot, c, kind, cut = v & 7, (v >> 3) & 3, (v >> 5) & 1, v >> 6
        return jnp.where(slot < CAP, ((c * CUTS + cut) * 2 + kind) * CAP + slot, -1)

    shape = (CUTS * 2 * slot_rows, ctx_count * size)
    order = (source(iota(shape, 0)) == iota(shape, 1)).astype(F32).astype(BF16)
    sorted_rows = dot(order, arrived).astype(BF16)

    def whole(kind):
        pieces = []
        for q in range(blocks):
            for cut in range(CUTS):
                first = (cut * 2 + kind) * slot_rows
                pieces.append(sorted_rows[first : first + slot_rows, q * part : (q + 1) * part])
        return jnp.concatenate(pieces, axis=1)

    expert_x, expert_dy = whole(0), whole(1)
    gate_pre = dot(expert_x, gate_ref[...])
    up_pre = dot(expert_x, up_ref[...])
    hidden_grad = dot_t(expert_dy, down_ref[...])
    sigmoid_gate = jax.nn.sigmoid(gate_pre)
    hidden = (gate_pre * sigmoid_gate * up_pre).astype(BF16)
    gate_grad = (
        hidden_grad * up_pre * sigmoid_gate * (1.0 + gate_pre * (1.0 - sigmoid_gate))
    ).astype(BF16)
    up_grad = (hidden_grad * gate_pre * sigmoid_gate).astype(BF16)
    out_term = dot(hidden, down_ref[...]).astype(BF16)
    input_term = (dot_t(gate_grad, gate_ref[...]) + dot_t(up_grad, up_ref[...])).astype(BF16)

    dp_count = out_ref.shape[0] // ctx_count
    step = width // dp_count
    groups = []
    for cut in range(CUTS):
        for term in (out_term, input_term):
            groups.append(
                jnp.concatenate(
                    [
                        term[:, d * step + cut * LANES : d * step + (cut + 1) * LANES]
                        for d in range(dp_count)
                    ],
                    axis=1,
                )
            )
    shape = (shape[1], shape[0])
    order = (source(iota(shape, 1)) == iota(shape, 0)).astype(F32).astype(BF16)
    leaving = dot(order, jnp.concatenate(groups, axis=0)).astype(BF16)
    for c in range(ctx_count):
        for d in range(dp_count):
            out_ref[c * dp_count + d] = leaving[
                c * size : (c + 1) * size, d * LANES : (d + 1) * LANES
            ]


def combine_kernel(ctx_count, mix_ref, got_ref, out_ref):
    dp_count = got_ref.shape[0] // ctx_count
    sums = []
    for c in range(ctx_count):
        total = got_ref[c * dp_count].astype(F32)
        for d in range(1, dp_count):
            total = total + got_ref[c * dp_count + d].astype(F32)
        sums.append(total)
    rows = jnp.concatenate(sums, axis=0).astype(BF16)
    out_ref[...] = dot(mix_ref[...], rows).astype(BF16).reshape(out_ref.shape)


def finish_kernel(got_ref, mixed_ref, grad_ref):
    total = jnp.sum(got_ref[...].astype(F32), axis=0)
    count = mixed_ref.shape[0]
    for cut in range(CUTS):
        lanes = slice(cut * LANES, (cut + 1) * LANES)
        first = cut * 2 * count
        mixed_ref[:, lanes] = total[first : first + count].astype(BF16)
        grad_ref[:, lanes] = total[first + count : first + 2 * count].astype(BF16)


def body(tokens, cotangent, routes, probs, w_gate, w_up, w_down):
    dp_count = lax.axis_size("ya") * lax.axis_size("yb")
    ctx_count = lax.axis_size("ctx")
    tp_count = lax.axis_size("za") * lax.axis_size("zb") * lax.axis_size("xh")
    _, own_rows, width = tokens.shape
    column = routes.shape[1]
    block = width // 4
    size = CUTS * 2 * CAP
    tok_rows = column // tp_count
    any_space = pl.BlockSpec(memory_space=pl.ANY)
    smem = pl.BlockSpec(memory_space=pltpu.SMEM)
    vmem = pl.BlockSpec(memory_space=pltpu.VMEM)
    place = jnp.stack([lax.axis_index("za"), lax.axis_index("zb"), lax.axis_index("xh")]).astype(I32)

    spread = pl.pallas_call(
        spread_kernel,
        out_shape=jax.ShapeDtypeStruct((dp_count, 2, own_rows, block), BF16),
        in_specs=[smem, any_space, any_space],
        out_specs=any_space,
        scratch_shapes=[pltpu.SemaphoreType.DMA((2 * dp_count,))],
        compiler_params=params(4),
        name="spread",
    )(place, tokens, cotangent)
    parts = lax.all_to_all(spread, DP, split_axis=0, concat_axis=0, tiled=True)
    parts = parts.reshape(dp_count, 2 * own_rows, block)

    pack, mix = pl.pallas_call(
        lambda *refs: selector_kernel(ctx_count, tp_count, *refs),
        out_shape=(
            jax.ShapeDtypeStruct((ctx_count * 2 * size, CUTS * 2 * column), BF16),
            jax.ShapeDtypeStruct((tp_count * CUTS * 2 * tok_rows, ctx_count * size), BF16),
        ),
        in_specs=[smem, vmem, vmem],
        out_specs=(vmem, vmem),
        compiler_params=params(8),
        cost_estimate=pl.CostEstimate(flops=60_000_000, bytes_accessed=600_000, transcendentals=0),
        name="selectors",
    )(place, routes[0].T, probs[0].T)

    packed = pl.pallas_call(
        pack_kernel,
        out_shape=jax.ShapeDtypeStruct((ctx_count * 4, size, block // CUTS), BF16),
        in_specs=[vmem, vmem],
        out_specs=vmem,
        compiler_params=params(8),
        name="pack",
    )(pack, parts)
    moved = lax.all_to_all(packed, ("ctx", "yb", "zb"), split_axis=0, concat_axis=0, tiled=True)

    terms = pl.pallas_call(
        lambda *refs: expert_kernel(ctx_count, *refs),
        out_shape=jax.ShapeDtypeStruct((ctx_count * dp_count, size, LANES), BF16),
        in_specs=[vmem] * 4,
        out_specs=vmem,
        compiler_params=params(16),
        name="expert",
    )(moved, w_gate[0], w_up[0], w_down[0])
    back = lax.all_to_all(terms, ("ctx",) + DP, split_axis=0, concat_axis=0, tiled=True)

    per_owner = pl.pallas_call(
        lambda *refs: combine_kernel(ctx_count, *refs),
        out_shape=jax.ShapeDtypeStruct((tp_count, CUTS * 2 * tok_rows, LANES), BF16),
        in_specs=[vmem] * 2,
        out_specs=vmem,
        compiler_params=params(8),
        name="combine",
    )(mix, back)
    got = lax.all_to_all(per_owner, TP, split_axis=0, concat_axis=0, tiled=True)

    out = jax.ShapeDtypeStruct((tok_rows, width // dp_count), BF16)
    mixed, input_grad = pl.pallas_call(
        finish_kernel,
        out_shape=(out, out),
        in_specs=[vmem],
        out_specs=(vmem, vmem),
        compiler_params=params(4),
        name="finish",
    )(got)
    return mixed[None], input_grad[None]


def solution(mesh):
    dp_count, ctx_count, tp_count = (mesh.shape[axis] for axis in ("dp", "ctx", "tp"))
    z_count = tp_count // X_PARTS
    fine = Mesh(
        mesh.devices.reshape(dp_count // 2, 2, ctx_count, z_count // 2, 2, X_PARTS),
        ("ya", "yb", "ctx", "za", "zb", "xh"),
    )
    experts = ("ctx",) + TP
    placed = (
        P("ctx", DP, None),
        P("ctx", DP, None),
        P("ctx", None, None),
        P("ctx", None, None),
        P(experts, None, DP),
        P(experts, None, DP),
        P(experts, DP, None),
    )
    return jax.shard_map(
        body,
        mesh=fine,
        in_specs=placed,
        out_specs=(P("ctx", TP, DP), P("ctx", TP, DP)),
        check_vma=False,
    )
```

time: 99.4 us -> 91.7 us (0.923)
  the two profiles are of different devices: /device:TPU:2 before, /device:TPU:1 now
where the time goes in v2:
time: 91.7 us; the launch traced here: 90 us
  blocking collectives  64 us (70%)
  starting transfers between devices  8.25 us (9%)
  waiting for transfers between devices  7.89 us (9%)
  Pallas kernels  6.22 us (7%)
  local copies, waits for them, and re-layouts  2.92 us (3%)
    all_to_all x1, blocking collectives, body(): got = lax.all_to_all(per_owner, TP, split_axis=0, concat_axis=0, tiled=True)  26.7 us
    all_to_all x1, blocking collectives, body(): lax.all_to_all(packed, ('ctx', 'yb', 'zb'), split_axis=0, concat_axis=0,...  21.3 us
    all_to_all x1, blocking collectives, body(): lax.all_to_all(terms, ('ctx',) + DP, split_axis=0, concat_axis=0, tiled=T...  15.9 us
    all_to_all x1, starting transfers between devices, body(): parts = lax.all_to_all(spread, DP, split_axis=0, concat_axis=0, tiled=True)  8.25 us
    all_to_all x1, waiting for transfers between devices, body(): parts = lax.all_to_all(spread, DP, split_axis=0, concat_axis=0, tiled=True)  7.89 us
    unnamed x14, local copies, waits for them, and re-layouts  2.92 us
    pallas_call x1, Pallas kernels, body(): pl.pallas_call(lambda *refs: expert_kernel(ctx_count, *refs), out_shape=j...  2.29 us
  transfers between devices with their start and end apart: 1, of which 1 were waited for; matrix products, arithmetic and copies ran while one was open for 0% of the time, Pallas kernels for 2%

profile of v2, /device:TPU:1, one launch (start us, length us, event | category | flops | bytes accessed | tf_op | source)
XLA Modules:
  0.0 90.0 jit_solution(463887425240423674)
XLA Ops:
  0.6 0.1 pad_add_fusion.refs_0_.at_ref
  0.7 0.0 copy-start.3
  0.7 0.8 copy-done.3
  1.6 0.0 copy-start.4
  1.6 0.8 copy-done.4
  2.4 0.0 copy-start.5
  2.4 1.4 %spread.1 = bf16[8,2,8,1024]{3,2,1,0:T(8,128)(2,1)} custom-call(s32[3]{0:T(128)S(1)} %pad_add_fusion.refs_0_.at_ref, bf16[1,8,4096]{2,1,0:T(8,128)(2,1)S(1)} %copy-done.3, bf16[1,8,4096]{2,1,0:T(8,128)(2,1)S(1)} %copy-done.4), custom_call_target="tpu_custom_call" | custom-call | tf_op jit(solution)/shard_map/spread/pallas_call | solution.py:242
  3.8 0.0 copy-start.1
  3.8 8.2 %all-to-all-start = ((bf16[8,2,8,1024]{3,2,1,0:T(8,128)(2,1)}), bf16[8,2,8,1024]{3,2,1,0:T(8,128)(2,1)S(1)}, u32[]{:S(2)}, u32[]{:S(2)}) async-start(bf16[8,2,8,1024]{3,2,1,0:T(8,128)(2,1)} %spread.1), calls=%async_computation | async-start | bytes 524288 | tf_op jit(solution)/shard_map/all_to_all | solution.py:251
  12.1 0.0 copy-done.5
  12.1 0.0 copy-done.6
  12.1 1.4 %selectors.1 = (bf16[384,512]{1,0:T(8,128)(2,1)S(1)}, bf16[512,192]{1,0:T(8,128)(2,1)S(1)}) custom-call(s32[3]{0:T(128)S(1)} %pad_add_fusion.refs_0_.at_ref, s32[8,64]{1,0:T(8,128)S(1)} %bitcast.19, bf16[8,64]{1,0:T(8,128)(2,1)S(1)} %bitcast.20), custom_call_target="tpu_custom_call" | custom-call | flops 60000000 | bytes 600000 | tf_op jit(solution)/shard_map/selectors/pallas_call | solution.py:254
  13.5 7.9 %all-to-all-done = bf16[8,2,8,1024]{3,2,1,0:T(8,128)(2,1)S(1)} async-done(((bf16[8,2,8,1024]{3,2,1,0:T(8,128)(2,1)}), bf16[8,2,8,1024]{3,2,1,0:T(8,128)(2,1)S(1)}, u32[]{:S(2)}, u32[]{:S(2)}) %all-to-all-start) | async-done | bytes 262176 | tf_op jit(solution)/shard_map/all_to_all | solution.py:251
  21.4 0.3 pack.1
  21.7 21.3 %all_to_all.20.refs_0_ = bf16[16,48,256]{2,1,0:T(8,128)(2,1)S(1)} all-to-all(bf16[16,48,256]{2,1,0:T(8,128)(2,1)S(1)} %pack.1), channel_id=1, replica_groups=mesh['ya'=4,'yb'=2,'ctx'=4,'za'=4,'zb'=2,'xh'=4] {'ctx','yb','zb'}, dimensions={0} | all-to-all | bytes 786432 | tf_op jit(solution)/shard_map/all_to_all | solution.py:275
  43.0 0.0 copy-done.1
  43.0 0.0 copy-done
  43.0 0.0 copy-start.2
  43.0 1.2 %copy-done.2 = bf16[1,128,4096]{2,1,0:T(8,128)(2,1)S(1)} copy-done((bf16[1,128,4096]{2,1,0:T(8,128)(2,1)S(1)}, bf16[1,128,4096]{2,1,0:T(8,128)(2,1)}, u32[]{:S(2)}) %copy-start.2) | copy-done | bytes 1048600
  44.2 2.3 %expert.1 = bf16[32,48,128]{2,1,0:T(8,128)(2,1)S(1)} custom-call(bf16[16,48,256]{2,1,0:T(8,128)(2,1)S(1)} %all_to_all.20.refs_0_, bf16[4096,128]{1,0:T(8,128)(2,1)S(1)} %bitcast.16, bf16[4096,128]{1,0:T(8,128)(2,1)S(1)} %bitcast.17, bf16[128,4096]{1,0:T(8,128)(2,1)S(1)} %bitcast.18), custom_call_target="tpu_custom_call" | custom-call | tf_op jit(solution)/shard_map/expert/pallas_call | solution.py:277
  46.5 15.9 %all_to_all.21.refs_1_ = bf16[32,48,128]{2,1,0:T(8,128)(2,1)S(1)} all-to-all(bf16[32,48,128]{2,1,0:T(8,128)(2,1)S(1)} %expert.1), channel_id=1, replica_groups=mesh['ya'=4,'yb'=2,'ctx'=4,'za'=4,'zb'=2,'xh'=4] {'ctx','ya','yb'}, dimensions={0} | all-to-all | bytes 786432 | tf_op jit(solution)/shard_map/all_to_all | solution.py:285
  62.4 0.2 combine.1
  62.7 26.7 %all_to_all.22.got_ref = bf16[32,16,128]{2,1,0:T(8,128)(2,1)S(1)} all-to-all(bf16[32,16,128]{2,1,0:T(8,128)(2,1)S(1)} %combine.1), channel_id=1, replica_groups=mesh['ya'=4,'yb'=2,'ctx'=4,'za'=4,'zb'=2,'xh'=4] {'za','zb','xh'}, dimensions={0} | all-to-all | bytes 262144 | tf_op jit(solution)/shard_map/all_to_all | solution.py:295
  89.4 0.6 finish.1
  (2 shorter events, 0.0 us)
Async XLA Ops:
  0.7 0.8 copy-start.3
  1.6 0.8 copy-start.4
  2.4 9.7 %copy-start.5 = (s32[1,64,8]{1,2,0:T(8,128)S(1)}, s32[1,64,8]{1,2,0:T(8,128)}, u32[]{:S(2)}) copy-start(s32[1,64,8]{1,2,0:T(8,128)} %param.9) | copy-start | bytes 6148
  2.4 9.7 %copy-start.6 = (bf16[1,64,8]{1,2,0:T(8,128)(2,1)S(1)}, bf16[1,64,8]{1,2,0:T(8,128)(2,1)}, u32[]{:S(2)}) copy-start(bf16[1,64,8]{1,2,0:T(8,128)(2,1)} %param.10) | copy-start | bytes 3076
  3.8 39.2 %copy-start.1 = (bf16[1,4096,128]{2,1,0:T(8,128)(2,1)S(1)}, bf16[1,4096,128]{2,1,0:T(8,128)(2,1)}, u32[]{:S(2)}) copy-start(bf16[1,4096,128]{2,1,0:T(8,128)(2,1)} %param.12) | copy-start | bytes 3145732
  3.8 17.6 %all-to-all-start = ((bf16[8,2,8,1024]{3,2,1,0:T(8,128)(2,1)}), bf16[8,2,8,1024]{3,2,1,0:T(8,128)(2,1)S(1)}, u32[]{:S(2)}, u32[]{:S(2)}) async-start(bf16[8,2,8,1024]{3,2,1,0:T(8,128)(2,1)} %spread.1), calls=%async_computation | async-start | bytes 524288 | tf_op jit(solution)/shard_map/all_to_all | solution.py:251
  12.1 30.9 %copy-start = (bf16[1,4096,128]{2,1,0:T(8,128)(2,1)S(1)}, bf16[1,4096,128]{2,1,0:T(8,128)(2,1)}, u32[]{:S(2)}) copy-start(bf16[1,4096,128]{2,1,0:T(8,128)(2,1)} %param.11) | copy-start | bytes 3145732
  43.0 1.2 %copy-start.2 = (bf16[1,128,4096]{2,1,0:T(8,128)(2,1)S(1)}, bf16[1,128,4096]{2,1,0:T(8,128)(2,1)}, u32[]{:S(2)}) copy-start(bf16[1,128,4096]{2,1,0:T(8,128)(2,1)} %param.13) | copy-start | bytes 3145732

commit v3 on v2

--- a/solution.py
+++ b/solution.py
@@ -35,29 +35,44 @@
     )
 
 
+def in_hbm(v):
+    return pltpu.with_memory_space_constraint(v, pltpu.HBM)
+
+
 def params(mib):
     return pltpu.CompilerParams(vmem_limit_bytes=mib << 20)
 
 
-def spread_kernel(at_ref, tok_ref, cot_ref, out_ref, sems):
+def spread_kernel(at_ref, tok_ref, cot_ref, out_ref, held, sems):
     own = at_ref[1]
     block = out_ref.shape[3]
     copies = []
-    for d in range(out_ref.shape[0]):
+    for yb in range(2):
         for kind, ref in enumerate((tok_ref, cot_ref)):
-            start = pl.multiple_of(((d % 2) * 2 + own) * block, block)
+            start = pl.multiple_of((yb * 2 + own) * block, block)
             copies.append(
                 pltpu.make_async_copy(
-                    ref.at[0, :, pl.ds(start, block)], out_ref.at[d, kind], sems.at[2 * d + kind]
+                    ref.at[0, :, pl.ds(start, block)], held.at[yb, kind], sems.at[2 * yb + kind]
                 )
             )
     for copy in copies:
         copy.start()
+    for yb in range(2):
+        for kind in range(2):
+            copies[2 * yb + kind].wait()
+            value = held[yb, kind]
+            for d in range(yb, out_ref.shape[0], 2):
+                out_ref[d, kind] = value
+
+
+def selector_kernel(ctx_count, tp_count, *refs):
+    at_ref, routes_ref, probs_ref, *weights, pack_ref, mix_ref = refs[:8]
+    copies = [
+        pltpu.make_async_copy(ref.at[0], held, refs[11].at[i])
+        for i, (ref, held) in enumerate(zip(weights, refs[8:11]))
+    ]
     for copy in copies:
-        copy.wait()
-
-
-def selector_kernel(ctx_count, tp_count, at_ref, routes_ref, probs_ref, pack_ref, mix_ref):
+        copy.start()
     za, zb, xh = at_ref[0], at_ref[1], at_ref[2]
     top, column = routes_ref.shape
     columns = 2 * column
@@ -122,6 +137,8 @@
     row, col = iota(full.shape, 0), sixth(iota(full.shape, 1))
     same = (((row >> 1) & 1) == (col & 1)) & (((row >> 2) & 3) == ((col >> 1) & 3))
     mix_ref[...] = jnp.where(same, full, 0.0).astype(BF16)
+    for copy in copies:
+        copy.wait()
 
 
 def pack_kernel(pack_ref, got_ref, out_ref):
@@ -241,28 +258,34 @@
 
     spread = pl.pallas_call(
         spread_kernel,
-        out_shape=jax.ShapeDtypeStruct((dp_count, 2, own_rows, block), BF16),
+        out_shape=pltpu.VMEM((dp_count, 2, own_rows, block), BF16),
         in_specs=[smem, any_space, any_space],
-        out_specs=any_space,
-        scratch_shapes=[pltpu.SemaphoreType.DMA((2 * dp_count,))],
+        out_specs=vmem,
+        scratch_shapes=[
+            pltpu.VMEM((2, 2, own_rows, block), BF16),
+            pltpu.SemaphoreType.DMA((4,)),
+        ],
         compiler_params=params(4),
         name="spread",
-    )(place, tokens, cotangent)
+    )(place, in_hbm(tokens), in_hbm(cotangent))
     parts = lax.all_to_all(spread, DP, split_axis=0, concat_axis=0, tiled=True)
     parts = parts.reshape(dp_count, 2 * own_rows, block)
 
-    pack, mix = pl.pallas_call(
+    weights = (w_gate, w_up, w_down)
+    pack, mix, *held = pl.pallas_call(
         lambda *refs: selector_kernel(ctx_count, tp_count, *refs),
         out_shape=(
             jax.ShapeDtypeStruct((ctx_count * 2 * size, CUTS * 2 * column), BF16),
             jax.ShapeDtypeStruct((tp_count * CUTS * 2 * tok_rows, ctx_count * size), BF16),
+            *(pltpu.VMEM(weight.shape[1:], BF16) for weight in weights),
         ),
-        in_specs=[smem, vmem, vmem],
-        out_specs=(vmem, vmem),
+        in_specs=[smem, vmem, vmem] + [any_space] * 3,
+        out_specs=(vmem,) * 5,
+        scratch_shapes=[pltpu.SemaphoreType.DMA((3,))],
         compiler_params=params(8),
-        cost_estimate=pl.CostEstimate(flops=60_000_000, bytes_accessed=600_000, transcendentals=0),
+        cost_estimate=pl.CostEstimate(flops=60_000_000, bytes_accessed=7_000_000, transcendentals=0),
         name="selectors",
-    )(place, routes[0].T, probs[0].T)
+    )(place, routes[0].T, probs[0].T, *(in_hbm(weight) for weight in weights))
 
     packed = pl.pallas_call(
         pack_kernel,
@@ -281,7 +304,7 @@
         out_specs=vmem,
         compiler_params=params(16),
         name="expert",
-    )(moved, w_gate[0], w_up[0], w_down[0])
+    )(moved, *held)
     back = lax.all_to_all(terms, ("ctx",) + DP, split_axis=0, concat_axis=0, tiled=True)
 
     per_owner = pl.pallas_call(

time: 91.7 us -> 90.6 us (0.988)
  waiting for transfers between devices: 7.89 us -> 4.8 us
  Pallas kernels: 6.22 us -> 7.88 us
    all_to_all x1, waiting for transfers between devices: 7.89 us -> 4.8 us  [body(): parts = lax.all_to_all(spread, DP, split_axis=0, concat_axis=0, tiled=True)]
    pallas_call x1, Pallas kernels: 1.41 us -> 2.42 us  [body(): pl.pallas_call(lambda *refs: selector_kernel(ctx_count, tp_count, *refs),...]
    unnamed x14 -> x12, local copies, waits for them, and re-layouts: 2.92 us -> 3.09 us
  transfers between devices with their start and end apart: 1 -> 1, of which waited for: 1 -> 1; matrix products, arithmetic and copies ran while one was open for 0% -> 0% of each run, Pallas kernels for 2% -> 3%
where the time goes in v3:
time: 90.6 us; the launch traced here: 88.8 us
  blocking collectives  64.2 us (71%)
  starting transfers between devices  8.12 us (9%)
  Pallas kernels  7.88 us (9%)
  waiting for transfers between devices  4.8 us (5%)
  local copies, waits for them, and re-layouts  3.09 us (3%)
    all_to_all x1, blocking collectives, body(): got = lax.all_to_all(per_owner, TP, split_axis=0, concat_axis=0, tiled=True)  26.8 us
    all_to_all x1, blocking collectives, body(): lax.all_to_all(packed, ('ctx', 'yb', 'zb'), split_axis=0, concat_axis=0,...  21.3 us
    all_to_all x1, blocking collectives, body(): lax.all_to_all(terms, ('ctx',) + DP, split_axis=0, concat_axis=0, tiled=T...  16.1 us
    all_to_all x1, starting transfers between devices, body(): parts = lax.all_to_all(spread, DP, split_axis=0, concat_axis=0, tiled=True)  8.12 us
    all_to_all x1, waiting for transfers between devices, body(): parts = lax.all_to_all(spread, DP, split_axis=0, concat_axis=0, tiled=True)  4.8 us
    unnamed x12, local copies, waits for them, and re-layouts  3.09 us
    pallas_call x1, Pallas kernels, body(): pl.pallas_call(lambda *refs: selector_kernel(ctx_count, tp_count, *refs),...  2.42 us
    pallas_call x1, Pallas kernels, body(): pl.pallas_call(lambda *refs: expert_kernel(ctx_count, *refs), out_shape=j...  2.28 us
  transfers between devices with their start and end apart: 1, of which 1 were waited for; matrix products, arithmetic and copies ran while one was open for 0% of the time, Pallas kernels for 3%

profile of v3, /device:TPU:1, one launch (start us, length us, event | category | flops | bytes accessed | tf_op | source)
XLA Modules:
  0.0 88.8 jit_solution(17628308220324657422)
XLA Ops:
  0.6 0.1 pad_add_fusion.refs_0_.at_ref
  0.7 2.1 %spread.1 = bf16[8,2,8,1024]{3,2,1,0:T(8,128)(2,1)} custom-call(s32[3]{0:T(128)S(1)} %pad_add_fusion.refs_0_.at_ref, bf16[1,8,4096]{2,1,0:T(8,128)(2,1)} %tok_ref.1, bf16[1,8,4096]{2,1,0:T(8,128)(2,1)} %cot_ref.1), custom_call_target="tpu_custom_call" | custom-call | tf_op jit(solution)/shard_map/spread/pallas_call | solution.py:259
  2.8 0.0 copy-start.4
  2.8 8.1 %all-to-all-start = ((bf16[8,2,8,1024]{3,2,1,0:T(8,128)(2,1)}), bf16[8,2,8,1024]{3,2,1,0:T(8,128)(2,1)S(1)}, u32[]{:S(2)}, u32[]{:S(2)}) async-start(bf16[8,2,8,1024]{3,2,1,0:T(8,128)(2,1)} %spread.1), calls=%async_computation | async-start | bytes 524288 | tf_op jit(solution)/shard_map/all_to_all | solution.py:271
  10.9 0.0 copy-start.5
  10.9 0.0 copy-done.4
  10.9 0.7 copy-done.5
  11.6 2.4 %selectors.1 = (bf16[384,512]{1,0:T(8,128)(2,1)S(1)}, bf16[512,192]{1,0:T(8,128)(2,1)S(1)}, bf16[4096,128]{1,0:T(8,128)(2,1)S(1)}, bf16[4096,128]{1,0:T(8,128)(2,1)S(1)}, bf16[128,4096]{1,0:T(8,128)(2,1)S(1)}) custom-call(s32[3]{0:T(128)S(1)} %pad_add_fusion.refs_0_.at_ref, s32[8,64]{1,0:T(8,128)S(1)} %bitcast.13, bf16[8,64]{1,0:T(8,128)(2,1)S(1)} %bitcast.14, ...), custom_call_target="tpu_custom_call" | custom-call | flops 60000000 | bytes 7000000 | tf_op jit(solution)/shard_map/selectors/pallas_call | solution.py:275
  14.0 0.0 copy-start
  14.0 0.7 copy-done
  14.8 0.0 copy-start.2
  14.8 0.7 copy-done.2
  15.4 4.8 %all-to-all-done = bf16[8,2,8,1024]{3,2,1,0:T(8,128)(2,1)S(1)} async-done(((bf16[8,2,8,1024]{3,2,1,0:T(8,128)(2,1)}), bf16[8,2,8,1024]{3,2,1,0:T(8,128)(2,1)S(1)}, u32[]{:S(2)}, u32[]{:S(2)}) %all-to-all-start) | async-done | bytes 262176 | tf_op jit(solution)/shard_map/all_to_all | solution.py:271
  20.2 0.0 copy-start.1
  20.2 1.0 %copy-done.1 = bf16[384,512]{1,0:T(8,128)(2,1)S(1)} copy-done((bf16[384,512]{1,0:T(8,128)(2,1)S(1)}, bf16[384,512]{1,0:T(8,128)(2,1)}, u32[]{:S(2)}) %copy-start.1) | copy-done | bytes 393240
  21.2 0.3 pack.1
  21.5 21.3 %all_to_all.20.refs_0_ = bf16[16,48,256]{2,1,0:T(8,128)(2,1)S(1)} all-to-all(bf16[16,48,256]{2,1,0:T(8,128)(2,1)S(1)} %pack.1), channel_id=1, replica_groups=mesh['ya'=4,'yb'=2,'ctx'=4,'za'=4,'zb'=2,'xh'=4] {'ctx','yb','zb'}, dimensions={0} | all-to-all | bytes 786432 | tf_op jit(solution)/shard_map/all_to_all | solution.py:298
  42.8 2.3 %expert.1 = bf16[32,48,128]{2,1,0:T(8,128)(2,1)S(1)} custom-call(bf16[16,48,256]{2,1,0:T(8,128)(2,1)S(1)} %all_to_all.20.refs_0_, bf16[4096,128]{1,0:T(8,128)(2,1)S(1)} %get-tuple-element.11.refs_1_, bf16[4096,128]{1,0:T(8,128)(2,1)S(1)} %get-tuple-element.12.refs_2_, bf16[128,4096]{1,0:T(8,128)(2,1)S(1)} %get-tuple-element.13.refs_3_), custom_call_target="tpu_custom_call" | custom-call | tf_op jit(solution)/shard_map/expert/pallas_call | solution.py:300
  45.1 0.0 copy-start.3
  45.1 16.1 %all_to_all.21.refs_1_ = bf16[32,48,128]{2,1,0:T(8,128)(2,1)S(1)} all-to-all(bf16[32,48,128]{2,1,0:T(8,128)(2,1)S(1)} %expert.1), channel_id=1, replica_groups=mesh['ya'=4,'yb'=2,'ctx'=4,'za'=4,'zb'=2,'xh'=4] {'ctx','ya','yb'}, dimensions={0} | all-to-all | bytes 786432 | tf_op jit(solution)/shard_map/all_to_all | solution.py:308
  61.2 0.0 copy-done.3
  61.2 0.2 combine.1
  61.4 26.8 %all_to_all.22.got_ref = bf16[32,16,128]{2,1,0:T(8,128)(2,1)S(1)} all-to-all(bf16[32,16,128]{2,1,0:T(8,128)(2,1)S(1)} %combine.1), channel_id=1, replica_groups=mesh['ya'=4,'yb'=2,'ctx'=4,'za'=4,'zb'=2,'xh'=4] {'za','zb','xh'}, dimensions={0} | all-to-all | bytes 262144 | tf_op jit(solution)/shard_map/all_to_all | solution.py:318
  88.2 0.6 finish.1
Async XLA Ops:
  2.8 8.1 %copy-start.4 = (s32[1,64,8]{1,2,0:T(8,128)S(1)}, s32[1,64,8]{1,2,0:T(8,128)}, u32[]{:S(2)}) copy-start(s32[1,64,8]{1,2,0:T(8,128)} %param.9) | copy-start | bytes 6148
  2.8 17.5 %all-to-all-start = ((bf16[8,2,8,1024]{3,2,1,0:T(8,128)(2,1)}), bf16[8,2,8,1024]{3,2,1,0:T(8,128)(2,1)S(1)}, u32[]{:S(2)}, u32[]{:S(2)}) async-start(bf16[8,2,8,1024]{3,2,1,0:T(8,128)(2,1)} %spread.1), calls=%async_computation | async-start | bytes 524288 | tf_op jit(solution)/shard_map/all_to_all | solution.py:271
  10.9 0.7 copy-start.5
  14.0 0.7 copy-start
  14.8 0.7 copy-start.2
  20.2 1.0 %copy-start.1 = (bf16[384,512]{1,0:T(8,128)(2,1)S(1)}, bf16[384,512]{1,0:T(8,128)(2,1)}, u32[]{:S(2)}) copy-start(bf16[384,512]{1,0:T(8,128)(2,1)} %copy-done) | copy-start | bytes 1179652
  45.1 16.1 %copy-start.3 = (bf16[512,192]{1,0:T(8,128)(2,1)S(1)}, bf16[512,192]{1,0:T(8,128)(2,1)}, u32[]{:S(2)}) copy-start(bf16[512,192]{1,0:T(8,128)(2,1)} %copy-done.2) | copy-start | bytes 589828

commit v4 on v2

--- a/solution.py
+++ b/solution.py
@@ -35,30 +35,16 @@
     )
 
 
+def in_hbm(v):
+    return pltpu.with_memory_space_constraint(v, pltpu.HBM)
+
+
 def params(mib):
     return pltpu.CompilerParams(vmem_limit_bytes=mib << 20)
 
 
-def spread_kernel(at_ref, tok_ref, cot_ref, out_ref, sems):
-    own = at_ref[1]
-    block = out_ref.shape[3]
-    copies = []
-    for d in range(out_ref.shape[0]):
-        for kind, ref in enumerate((tok_ref, cot_ref)):
-            start = pl.multiple_of(((d % 2) * 2 + own) * block, block)
-            copies.append(
-                pltpu.make_async_copy(
-                    ref.at[0, :, pl.ds(start, block)], out_ref.at[d, kind], sems.at[2 * d + kind]
-                )
-            )
-    for copy in copies:
-        copy.start()
-    for copy in copies:
-        copy.wait()
-
-
-def selector_kernel(ctx_count, tp_count, at_ref, routes_ref, probs_ref, pack_ref, mix_ref):
-    za, zb, xh = at_ref[0], at_ref[1], at_ref[2]
+def selectors(ctx_count, tp_count, place, routes_ref, probs_ref, pack_ref, mix_ref):
+    za, zb, xh = place
     top, column = routes_ref.shape
     columns = 2 * column
     experts = ctx_count * tp_count
@@ -122,6 +108,40 @@
     row, col = iota(full.shape, 0), sixth(iota(full.shape, 1))
     same = (((row >> 1) & 1) == (col & 1)) & (((row >> 2) & 3) == ((col >> 1) & 3))
     mix_ref[...] = jnp.where(same, full, 0.0).astype(BF16)
+
+
+def first_kernel(
+    ctx_count, tp_count, tok_ref, cot_ref, routes_ref, probs_ref, weight_ref,
+    out_ref, pack_ref, mix_ref, weight_out, held, routes, probs, sems,
+):
+    za, zb, xh = (lax.axis_index(axis) for axis in TP)
+    block = out_ref.shape[3]
+    small = [
+        pltpu.make_async_copy(ref, to, sems.at[4 + i])
+        for i, (ref, to) in enumerate(((routes_ref, routes), (probs_ref, probs)))
+    ]
+    copies = []
+    for yb in range(2):
+        for kind, ref in enumerate((tok_ref, cot_ref)):
+            start = pl.multiple_of((yb * 2 + zb) * block, block)
+            copies.append(
+                pltpu.make_async_copy(
+                    ref.at[0, :, pl.ds(start, block)], held.at[yb, kind], sems.at[2 * yb + kind]
+                )
+            )
+    weight_copy = pltpu.make_async_copy(weight_ref.at[0], weight_out, sems.at[6])
+    for copy in small + copies + [weight_copy]:
+        copy.start()
+    for copy in small:
+        copy.wait()
+    selectors(ctx_count, tp_count, (za, zb, xh), routes, probs, pack_ref, mix_ref)
+    for yb in range(2):
+        for kind in range(2):
+            copies[2 * yb + kind].wait()
+            value = held[yb, kind]
+            for d in range(yb, out_ref.shape[0], 2):
+                out_ref[d, kind] = value
+    weight_copy.wait()
 
 
 def pack_kernel(pack_ref, got_ref, out_ref):
@@ -230,39 +250,34 @@
     ctx_count = lax.axis_size("ctx")
     tp_count = lax.axis_size("za") * lax.axis_size("zb") * lax.axis_size("xh")
     _, own_rows, width = tokens.shape
-    column = routes.shape[1]
+    column, top = routes.shape[1:]
     block = width // 4
     size = CUTS * 2 * CAP
     tok_rows = column // tp_count
     any_space = pl.BlockSpec(memory_space=pl.ANY)
-    smem = pl.BlockSpec(memory_space=pltpu.SMEM)
     vmem = pl.BlockSpec(memory_space=pltpu.VMEM)
-    place = jnp.stack([lax.axis_index("za"), lax.axis_index("zb"), lax.axis_index("xh")]).astype(I32)
-
-    spread = pl.pallas_call(
-        spread_kernel,
-        out_shape=jax.ShapeDtypeStruct((dp_count, 2, own_rows, block), BF16),
-        in_specs=[smem, any_space, any_space],
-        out_specs=any_space,
-        scratch_shapes=[pltpu.SemaphoreType.DMA((2 * dp_count,))],
-        compiler_params=params(4),
-        name="spread",
-    )(place, tokens, cotangent)
+
+    spread, pack, mix, down = pl.pallas_call(
+        lambda *refs: first_kernel(ctx_count, tp_count, *refs),
+        out_shape=(
+            pltpu.VMEM((dp_count, 2, own_rows, block), BF16),
+            pltpu.VMEM((ctx_count * 2 * size, CUTS * 2 * column), BF16),
+            pltpu.VMEM((tp_count * CUTS * 2 * tok_rows, ctx_count * size), BF16),
+            pltpu.VMEM(w_down.shape[1:], BF16),
+        ),
+        in_specs=[any_space] * 5,
+        out_specs=(vmem,) * 4,
+        scratch_shapes=[
+            pltpu.VMEM((2, 2, own_rows, block), BF16),
+            pltpu.VMEM((top, column), I32),
+            pltpu.VMEM((top, column), BF16),
+            pltpu.SemaphoreType.DMA((7,)),
+        ],
+        compiler_params=params(8),
+        name="first",
+    )(*(in_hbm(v) for v in (tokens, cotangent, routes[0].T, probs[0].T, w_down)))
     parts = lax.all_to_all(spread, DP, split_axis=0, concat_axis=0, tiled=True)
     parts = parts.reshape(dp_count, 2 * own_rows, block)
-
-    pack, mix = pl.pallas_call(
-        lambda *refs: selector_kernel(ctx_count, tp_count, *refs),
-        out_shape=(
-            jax.ShapeDtypeStruct((ctx_count * 2 * size, CUTS * 2 * column), BF16),
-            jax.ShapeDtypeStruct((tp_count * CUTS * 2 * tok_rows, ctx_count * size), BF16),
-        ),
-        in_specs=[smem, vmem, vmem],
-        out_specs=(vmem, vmem),
-        compiler_params=params(8),
-        cost_estimate=pl.CostEstimate(flops=60_000_000, bytes_accessed=600_000, transcendentals=0),
-        name="selectors",
-    )(place, routes[0].T, probs[0].T)
 
     packed = pl.pallas_call(
         pack_kernel,
@@ -281,7 +296,7 @@
         out_specs=vmem,
         compiler_params=params(16),
         name="expert",
-    )(moved, w_gate[0], w_up[0], w_down[0])
+    )(moved, w_gate[0], w_up[0], down)
     back = lax.all_to_all(terms, ("ctx",) + DP, split_axis=0, concat_axis=0, tiled=True)
 
     per_owner = pl.pallas_call(

time: 91.7 us -> 88.8 us (0.968)
  blocking collectives: 64 us -> 81.5 us
  starting transfers between devices: 8.25 us -> 0 us
  waiting for transfers between devices: 7.89 us -> 0 us
  local copies, waits for them, and re-layouts: 2.92 us -> 0.01 us
  Pallas kernels: 6.22 us -> 5.07 us
    all_to_all x0 -> x1, blocking collectives: none -> 17.4 us  [body(): parts = lax.all_to_all(spread, DP, split_axis=0, concat_axis=0, tiled=True)]
    all_to_all x1 -> x0, starting transfers between devices: 8.25 us -> none  [body(): parts = lax.all_to_all(spread, DP, split_axis=0, concat_axis=0, tiled=True)]
    all_to_all x1 -> x0, waiting for transfers between devices: 7.89 us -> none  [body(): parts = lax.all_to_all(spread, DP, split_axis=0, concat_axis=0, tiled=True)]
    unnamed x14 -> x4, local copies, waits for them, and re-layouts: 2.92 us -> 0.01 us
    pallas_call x2 -> x1, Pallas kernels: 2.81 us -> 1.66 us  [body(): pl.pallas_call(lambda *refs: first_kernel(ctx_count, tp_count, *refs), ou...]
  transfers between devices with their start and end apart: 1 -> 0, of which waited for: 1 -> 0; matrix products, arithmetic and copies ran while one was open for 0% -> 0% of each run, Pallas kernels for 2% -> 0%
where the time goes in v4:
time: 88.8 us; the launch traced here: 87.2 us
  blocking collectives  81.5 us (92%)
  Pallas kernels  5.07 us (6%)
    all_to_all x1, blocking collectives, body(): got = lax.all_to_all(per_owner, TP, split_axis=0, concat_axis=0, tiled=True)  27.5 us
    all_to_all x1, blocking collectives, body(): lax.all_to_all(packed, ('ctx', 'yb', 'zb'), split_axis=0, concat_axis=0,...  20.7 us
    all_to_all x1, blocking collectives, body(): parts = lax.all_to_all(spread, DP, split_axis=0, concat_axis=0, tiled=True)  17.4 us
    all_to_all x1, blocking collectives, body(): lax.all_to_all(terms, ('ctx',) + DP, split_axis=0, concat_axis=0, tiled=T...  15.9 us
    pallas_call x1, Pallas kernels, body(): pl.pallas_call(lambda *refs: expert_kernel(ctx_count, *refs), out_shape=j...  2.29 us

profile of v4, /device:TPU:1, one launch (start us, length us, event | category | flops | bytes accessed | tf_op | source)
XLA Modules:
  0.0 87.2 jit_solution(6604091176977618916)
XLA Ops:
  0.6 1.7 %first.1 = (bf16[8,2,8,1024]{3,2,1,0:T(8,128)(2,1)S(1)}, bf16[384,512]{1,0:T(8,128)(2,1)S(1)}, bf16[512,192]{1,0:T(8,128)(2,1)S(1)}, bf16[128,4096]{1,0:T(8,128)(2,1)S(1)}) custom-call(bf16[1,8,4096]{2,1,0:T(8,128)(2,1)} %refs_0_.1, bf16[1,8,4096]{2,1,0:T(8,128)(2,1)} %refs_1_.1, s32[8,64]{1,0:T(8,128)} %bitcast.14, bf16[8,64]{1,0:T(8,128)(2,1)} %bitcast.15, ...), custom_call_target="tpu_custom_call" | custom-call | tf_op jit(solution)/shard_map/first/pallas_call | solution.py:260
  2.3 0.0 copy-start.1
  2.3 17.4 %all_to_all.20 = bf16[8,2,8,1024]{3,2,1,0:T(8,128)(2,1)S(1)} all-to-all(bf16[8,2,8,1024]{3,2,1,0:T(8,128)(2,1)S(1)} %get-tuple-element.10), channel_id=1, replica_groups=mesh['ya'=4,'yb'=2,'ctx'=4,'za'=4,'zb'=2,'xh'=4] {'ya','yb'}, dimensions={0} | all-to-all | bytes 524288 | tf_op jit(solution)/shard_map/all_to_all | solution.py:279
  19.7 0.0 copy-start
  19.7 0.3 pack.1
  19.9 20.7 %all_to_all.21.refs_0_ = bf16[16,48,256]{2,1,0:T(8,128)(2,1)S(1)} all-to-all(bf16[16,48,256]{2,1,0:T(8,128)(2,1)S(1)} %pack.1), channel_id=1, replica_groups=mesh['ya'=4,'yb'=2,'ctx'=4,'za'=4,'zb'=2,'xh'=4] {'ctx','yb','zb'}, dimensions={0} | all-to-all | bytes 786432 | tf_op jit(solution)/shard_map/all_to_all | solution.py:290
  40.7 0.0 copy-done.1
  40.7 0.0 copy-done
  40.7 2.3 %expert.1 = bf16[32,48,128]{2,1,0:T(8,128)(2,1)S(1)} custom-call(bf16[16,48,256]{2,1,0:T(8,128)(2,1)S(1)} %all_to_all.21.refs_0_, bf16[4096,128]{1,0:T(8,128)(2,1)S(1)} %bitcast.12, bf16[4096,128]{1,0:T(8,128)(2,1)S(1)} %bitcast.13, bf16[128,4096]{1,0:T(8,128)(2,1)S(1)} %get-tuple-element.11.refs_3_), custom_call_target="tpu_custom_call" | custom-call | tf_op jit(solution)/shard_map/expert/pallas_call | solution.py:292
  43.0 15.9 %all_to_all.22.refs_1_ = bf16[32,48,128]{2,1,0:T(8,128)(2,1)S(1)} all-to-all(bf16[32,48,128]{2,1,0:T(8,128)(2,1)S(1)} %expert.1), channel_id=1, replica_groups=mesh['ya'=4,'yb'=2,'ctx'=4,'za'=4,'zb'=2,'xh'=4] {'ctx','ya','yb'}, dimensions={0} | all-to-all | bytes 786432 | tf_op jit(solution)/shard_map/all_to_all | solution.py:300
  58.9 0.2 combine.1
  59.1 27.5 %all_to_all.23.got_ref = bf16[32,16,128]{2,1,0:T(8,128)(2,1)S(1)} all-to-all(bf16[32,16,128]{2,1,0:T(8,128)(2,1)S(1)} %combine.1), channel_id=1, replica_groups=mesh['ya'=4,'yb'=2,'ctx'=4,'za'=4,'zb'=2,'xh'=4] {'za','zb','xh'}, dimensions={0} | all-to-all | bytes 262144 | tf_op jit(solution)/shard_map/all_to_all | solution.py:310
  86.6 0.6 finish.1
Async XLA Ops:
  2.3 38.4 %copy-start.1 = (bf16[1,4096,128]{2,1,0:T(8,128)(2,1)S(1)}, bf16[1,4096,128]{2,1,0:T(8,128)(2,1)}, u32[]{:S(2)}) copy-start(bf16[1,4096,128]{2,1,0:T(8,128)(2,1)} %param.12) | copy-start | bytes 3145732
  19.7 21.0 %copy-start = (bf16[1,4096,128]{2,1,0:T(8,128)(2,1)S(1)}, bf16[1,4096,128]{2,1,0:T(8,128)(2,1)}, u32[]{:S(2)}) copy-start(bf16[1,4096,128]{2,1,0:T(8,128)(2,1)} %param.11) | copy-start | bytes 3145732

commit v5 on v4

--- a/solution.py
+++ b/solution.py
@@ -15,6 +15,16 @@
 ROWS = 8
 CUTS = 4
 LANES = 128
+
+
+def order_of(count, first):
+    return [(first + i) % count for i in range(count)]
+
+
+def exchange(v, axes, order):
+    return lax.all_to_all(
+        v, axes, split_axis=0, concat_axis=0, axis_index_groups=[order], tiled=True
+    )
 
 
 def sixth(v):
@@ -111,7 +121,7 @@
 
 
 def first_kernel(
-    ctx_count, tp_count, tok_ref, cot_ref, routes_ref, probs_ref, weight_ref,
+    ctx_count, tp_count, order, tok_ref, cot_ref, routes_ref, probs_ref, weight_ref,
     out_ref, pack_ref, mix_ref, weight_out, held, routes, probs, sems,
 ):
     za, zb, xh = (lax.axis_index(axis) for axis in TP)
@@ -139,32 +149,33 @@
         for kind in range(2):
             copies[2 * yb + kind].wait()
             value = held[yb, kind]
-            for d in range(yb, out_ref.shape[0], 2):
-                out_ref[d, kind] = value
+            for place, d in enumerate(order):
+                if d % 2 == yb:
+                    out_ref[place, kind] = value
     weight_copy.wait()
 
 
-def pack_kernel(pack_ref, got_ref, out_ref):
+def pack_kernel(order_in, order_out, pack_ref, got_ref, out_ref):
     sources, rows, block = got_ref.shape
-    got = got_ref[...].reshape(sources * rows, block)
+    got = jnp.concatenate([got_ref[order_in.index(d)] for d in range(sources)], axis=0)
     part = block // CUTS
     stacked = jnp.concatenate([got[:, c * part : (c + 1) * part] for c in range(CUTS)], axis=0)
     packed = dot(pack_ref[...], stacked).astype(BF16)
     size = out_ref.shape[1]
-    for to in range(out_ref.shape[0]):
+    for place, to in enumerate(order_out):
         c, zb = to >> 2, to & 1
         first = (c * 2 + zb) * size
-        out_ref[to] = packed[first : first + size]
-
-
-def expert_kernel(ctx_count, got_ref, gate_ref, up_ref, down_ref, out_ref):
+        out_ref[place] = packed[first : first + size]
+
+
+def expert_kernel(ctx_count, order_in, order_out, got_ref, gate_ref, up_ref, down_ref, out_ref):
     _, size, part = got_ref.shape
     blocks = got_ref.shape[0] // ctx_count
     width, hidden_rows = gate_ref.shape
     slot_rows = ctx_count * ROWS
     arrived = jnp.concatenate(
         [
-            jnp.concatenate([got_ref[c * blocks + q] for q in range(blocks)], axis=1)
+            jnp.concatenate([got_ref[order_in.index(c * blocks + q)] for q in range(blocks)], axis=1)
             for c in range(ctx_count)
         ],
         axis=0,
@@ -187,9 +198,10 @@
         return jnp.concatenate(pieces, axis=1)
 
     expert_x, expert_dy = whole(0), whole(1)
-    gate_pre = dot(expert_x, gate_ref[...])
-    up_pre = dot(expert_x, up_ref[...])
-    hidden_grad = dot_t(expert_dy, down_ref[...])
+    into = jnp.concatenate((gate_ref[...], up_ref[...]), axis=1)
+    pre = dot(expert_x, into)
+    gate_pre, up_pre = pre[:, :hidden_rows], pre[:, hidden_rows:]
+    hidden_grad = dot_t(down_ref[...], expert_dy).T
     sigmoid_gate = jax.nn.sigmoid(gate_pre)
     hidden = (gate_pre * sigmoid_gate * up_pre).astype(BF16)
     gate_grad = (
@@ -197,7 +209,7 @@
     ).astype(BF16)
     up_grad = (hidden_grad * gate_pre * sigmoid_gate).astype(BF16)
     out_term = dot(hidden, down_ref[...]).astype(BF16)
-    input_term = (dot_t(gate_grad, gate_ref[...]) + dot_t(up_grad, up_ref[...])).astype(BF16)
+    input_term = dot_t(jnp.concatenate((gate_grad, up_grad), axis=1), into).astype(BF16)
 
     dp_count = out_ref.shape[0] // ctx_count
     step = width // dp_count
@@ -216,23 +228,23 @@
     shape = (shape[1], shape[0])
     order = (source(iota(shape, 1)) == iota(shape, 0)).astype(F32).astype(BF16)
     leaving = dot(order, jnp.concatenate(groups, axis=0)).astype(BF16)
-    for c in range(ctx_count):
-        for d in range(dp_count):
-            out_ref[c * dp_count + d] = leaving[
-                c * size : (c + 1) * size, d * LANES : (d + 1) * LANES
-            ]
-
-
-def combine_kernel(ctx_count, mix_ref, got_ref, out_ref):
+    for place, to in enumerate(order_out):
+        c, d = to // dp_count, to % dp_count
+        out_ref[place] = leaving[c * size : (c + 1) * size, d * LANES : (d + 1) * LANES]
+
+
+def combine_kernel(ctx_count, order_in, order_out, mix_ref, got_ref, out_ref):
     dp_count = got_ref.shape[0] // ctx_count
     sums = []
     for c in range(ctx_count):
-        total = got_ref[c * dp_count].astype(F32)
+        total = got_ref[order_in.index(c * dp_count)].astype(F32)
         for d in range(1, dp_count):
-            total = total + got_ref[c * dp_count + d].astype(F32)
+            total = total + got_ref[order_in.index(c * dp_count + d)].astype(F32)
         sums.append(total)
     rows = jnp.concatenate(sums, axis=0).astype(BF16)
-    out_ref[...] = dot(mix_ref[...], rows).astype(BF16).reshape(out_ref.shape)
+    mixed = dot(mix_ref[...], rows).astype(BF16).reshape(out_ref.shape)
+    for place, to in enumerate(order_out):
+        out_ref[place] = mixed[to]
 
 
 def finish_kernel(got_ref, mixed_ref, grad_ref):
@@ -251,6 +263,12 @@
     tp_count = lax.axis_size("za") * lax.axis_size("zb") * lax.axis_size("xh")
     _, own_rows, width = tokens.shape
     column, top = routes.shape[1:]
+    orders = (
+        order_of(dp_count, 4),
+        order_of(ctx_count * 4, 1),
+        order_of(ctx_count * dp_count, 4),
+        order_of(tp_count, 30),
+    )
     block = width // 4
     size = CUTS * 2 * CAP
     tok_rows = column // tp_count
@@ -258,7 +276,7 @@
     vmem = pl.BlockSpec(memory_space=pltpu.VMEM)
 
     spread, pack, mix, down = pl.pallas_call(
-        lambda *refs: first_kernel(ctx_count, tp_count, *refs),
+        lambda *refs: first_kernel(ctx_count, tp_count, orders[0], *refs),
         out_shape=(
             pltpu.VMEM((dp_count, 2, own_rows, block), BF16),
             pltpu.VMEM((ctx_count * 2 * size, CUTS * 2 * column), BF16),
@@ -276,38 +294,38 @@
         compiler_params=params(8),
         name="first",
     )(*(in_hbm(v) for v in (tokens, cotangent, routes[0].T, probs[0].T, w_down)))
-    parts = lax.all_to_all(spread, DP, split_axis=0, concat_axis=0, tiled=True)
+    parts = exchange(spread, DP, orders[0])
     parts = parts.reshape(dp_count, 2 * own_rows, block)
 
     packed = pl.pallas_call(
-        pack_kernel,
+        lambda *refs: pack_kernel(orders[0], orders[1], *refs),
         out_shape=jax.ShapeDtypeStruct((ctx_count * 4, size, block // CUTS), BF16),
         in_specs=[vmem, vmem],
         out_specs=vmem,
         compiler_params=params(8),
         name="pack",
     )(pack, parts)
-    moved = lax.all_to_all(packed, ("ctx", "yb", "zb"), split_axis=0, concat_axis=0, tiled=True)
+    moved = exchange(packed, ("ctx", "yb", "zb"), orders[1])
 
     terms = pl.pallas_call(
-        lambda *refs: expert_kernel(ctx_count, *refs),
+        lambda *refs: expert_kernel(ctx_count, orders[1], orders[2], *refs),
         out_shape=jax.ShapeDtypeStruct((ctx_count * dp_count, size, LANES), BF16),
         in_specs=[vmem] * 4,
         out_specs=vmem,
         compiler_params=params(16),
         name="expert",
     )(moved, w_gate[0], w_up[0], down)
-    back = lax.all_to_all(terms, ("ctx",) + DP, split_axis=0, concat_axis=0, tiled=True)
+    back = exchange(terms, ("ctx",) + DP, orders[2])
 
     per_owner = pl.pallas_call(
-        lambda *refs: combine_kernel(ctx_count, *refs),
+        lambda *refs: combine_kernel(ctx_count, orders[2], orders[3], *refs),
         out_shape=jax.ShapeDtypeStruct((tp_count, CUTS * 2 * tok_rows, LANES), BF16),
         in_specs=[vmem] * 2,
         out_specs=vmem,
         compiler_params=params(8),
         name="combine",
     )(mix, back)
-    got = lax.all_to_all(per_owner, TP, split_axis=0, concat_axis=0, tiled=True)
+    got = exchange(per_owner, TP, orders[3])
 
     out = jax.ShapeDtypeStruct((tok_rows, width // dp_count), BF16)
     mixed, input_grad = pl.pallas_call(

time: 88.8 us -> 80.5 us (0.907); the launches traced: 87.2 us -> 80.3 us
  blocking collectives: 81.5 us -> 75 us
    all_to_all x4, blocking collectives: 81.5 us -> 75 us  [exchange(): lax.all_to_all(v, axes, split_axis=0, concat_axis=0, axis_index_groups=[o...]
where the time goes in v5:
time: 80.5 us; the launch traced here: 80.3 us
  blocking collectives  75 us (93%)
  Pallas kernels  4.58 us (6%)
    all_to_all x4, blocking collectives, exchange(): lax.all_to_all(v, axes, split_axis=0, concat_axis=0, axis_index_groups=[o...  75 us
    pallas_call x1, Pallas kernels, body(): pl.pallas_call(lambda *refs: expert_kernel(ctx_count, orders[1], orders[2...  1.8 us
    pallas_call x1, Pallas kernels, body(): pl.pallas_call(lambda *refs: first_kernel(ctx_count, tp_count, orders[0],...  1.66 us

profile of v5, /device:TPU:1, one launch (start us, length us, event | category | flops | bytes accessed | tf_op | source)
XLA Modules:
  0.0 80.3 jit_solution(2197622658068361790)
XLA Ops:
  0.6 1.7 %first.1 = (bf16[8,2,8,1024]{3,2,1,0:T(8,128)(2,1)S(1)}, bf16[384,512]{1,0:T(8,128)(2,1)S(1)}, bf16[512,192]{1,0:T(8,128)(2,1)S(1)}, bf16[128,4096]{1,0:T(8,128)(2,1)S(1)}) custom-call(bf16[1,8,4096]{2,1,0:T(8,128)(2,1)} %refs_0_.1, bf16[1,8,4096]{2,1,0:T(8,128)(2,1)} %refs_1_.1, s32[8,64]{1,0:T(8,128)} %bitcast.14, bf16[8,64]{1,0:T(8,128)(2,1)} %bitcast.15, ...), custom_call_target="tpu_custom_call" | custom-call | tf_op jit(solution)/shard_map/first/pallas_call | solution.py:278
  2.3 0.0 copy-start.1
  2.3 13.6 %all_to_all.20 = bf16[8,2,8,1024]{3,2,1,0:T(8,128)(2,1)S(1)} all-to-all(bf16[8,2,8,1024]{3,2,1,0:T(8,128)(2,1)S(1)} %get-tuple-element.10), channel_id=1, replica_groups={{512,640,768,896,0,128,256,384},{513,641,769,897,1,129,257,385},{514,64..., dimensions={0} | all-to-all | bytes 524288 | tf_op jit(solution)/shard_map/all_to_all | solution.py:25
  15.9 0.0 copy-start
  15.9 0.3 pack.1
  16.2 23.1 %all_to_all.21.refs_0_ = bf16[16,48,256]{2,1,0:T(8,128)(2,1)S(1)} all-to-all(bf16[16,48,256]{2,1,0:T(8,128)(2,1)S(1)} %pack.1), channel_id=1, replica_groups={{4,128,132,32,36,160,164,64,68,192,196,96,100,224,228,0},{5,129,133,33,..., dimensions={0} | all-to-all | bytes 786432 | tf_op jit(solution)/shard_map/all_to_all | solution.py:25
  39.2 0.0 copy-done.1
  39.3 0.0 copy-done
  39.3 1.8 %expert.1 = bf16[32,48,128]{2,1,0:T(8,128)(2,1)S(1)} custom-call(bf16[16,48,256]{2,1,0:T(8,128)(2,1)S(1)} %all_to_all.21.refs_0_, bf16[4096,128]{1,0:T(8,128)(2,1)S(1)} %bitcast.12, bf16[4096,128]{1,0:T(8,128)(2,1)S(1)} %bitcast.13, bf16[128,4096]{1,0:T(8,128)(2,1)S(1)} %get-tuple-element.11.refs_3_), custom_call_target="tpu_custom_call" | custom-call | tf_op jit(solution)/shard_map/expert/pallas_call | solution.py:310
  41.1 17.8 %all_to_all.22.refs_1_ = bf16[32,48,128]{2,1,0:T(8,128)(2,1)S(1)} all-to-all(bf16[32,48,128]{2,1,0:T(8,128)(2,1)S(1)} %expert.1), channel_id=1, replica_groups={{512,640,768,896,32,160,288,416,544,672,800,928,64,192,320,448,576,704,..., dimensions={0} | all-to-all | bytes 786432 | tf_op jit(solution)/shard_map/all_to_all | solution.py:25
  58.8 0.2 combine.1
  59.1 20.6 %all_to_all.23.got_ref = bf16[32,16,128]{2,1,0:T(8,128)(2,1)S(1)} all-to-all(bf16[32,16,128]{2,1,0:T(8,128)(2,1)S(1)} %combine.1), channel_id=1, replica_groups={{30,31,0,1,2,3,4,5,6,7,8,9,10,11,12,13,14,15,16,17,18,19,20,21,22,23,24..., dimensions={0} | all-to-all | bytes 262144 | tf_op jit(solution)/shard_map/all_to_all | solution.py:25
  79.6 0.6 finish.1
Async XLA Ops:
  2.3 37.0 %copy-start.1 = (bf16[1,4096,128]{2,1,0:T(8,128)(2,1)S(1)}, bf16[1,4096,128]{2,1,0:T(8,128)(2,1)}, u32[]{:S(2)}) copy-start(bf16[1,4096,128]{2,1,0:T(8,128)(2,1)} %param.12) | copy-start | bytes 3145732
  15.9 23.3 %copy-start = (bf16[1,4096,128]{2,1,0:T(8,128)(2,1)S(1)}, bf16[1,4096,128]{2,1,0:T(8,128)(2,1)}, u32[]{:S(2)}) copy-start(bf16[1,4096,128]{2,1,0:T(8,128)(2,1)} %param.11) | copy-start | bytes 3145732

commit v6 on v5

--- a/solution.py
+++ b/solution.py
@@ -15,10 +15,6 @@
 ROWS = 8
 CUTS = 4
 LANES = 128
-
-
-def order_of(count, first):
-    return [(first + i) % count for i in range(count)]
 
 
 def exchange(v, axes, order):
@@ -263,11 +259,19 @@
     tp_count = lax.axis_size("za") * lax.axis_size("zb") * lax.axis_size("xh")
     _, own_rows, width = tokens.shape
     column, top = routes.shape[1:]
+    dp_order = [(4 + step) % dp_count for step in (0, 4, 1, 5, 7, 3, 6, 2)]
     orders = (
-        order_of(dp_count, 4),
-        order_of(ctx_count * 4, 1),
-        order_of(ctx_count * dp_count, 4),
-        order_of(tp_count, 30),
+        dp_order,
+        [(1 + 7 * j) % (ctx_count * 4) for j in range(ctx_count * 4)],
+        [
+            (j // dp_count + 3 * j) % ctx_count * dp_count + (4 + 5 * j) % dp_count
+            for j in range(ctx_count * dp_count)
+        ],
+        [
+            (7 + 5 * j) % (tp_count // X_PARTS) * X_PARTS
+            + (2 + j // (tp_count // X_PARTS) + 3 * j) % X_PARTS
+            for j in range(tp_count)
+        ],
     )
     block = width // 4
     size = CUTS * 2 * CAP

time: 80.5 us -> 80.7 us (level)
  no operation moved by 1% of the time
where the time goes in v6:
time: 80.7 us; the launch traced here: 80.5 us
  blocking collectives  75.2 us (93%)
  Pallas kernels  4.58 us (6%)
    all_to_all x4, blocking collectives, exchange(): lax.all_to_all(v, axes, split_axis=0, concat_axis=0, axis_index_groups=[o...  75.2 us
    pallas_call x1, Pallas kernels, body(): pl.pallas_call(lambda *refs: expert_kernel(ctx_count, orders[1], orders[2...  1.8 us
    pallas_call x1, Pallas kernels, body(): pl.pallas_call(lambda *refs: first_kernel(ctx_count, tp_count, orders[0],...  1.66 us

profile of v6, /device:TPU:1, one launch (start us, length us, event | category | flops | bytes accessed | tf_op | source)
XLA Modules:
  0.0 80.5 jit_solution(3072211701992440774)
XLA Ops:
  0.6 1.7 %first.1 = (bf16[8,2,8,1024]{3,2,1,0:T(8,128)(2,1)S(1)}, bf16[384,512]{1,0:T(8,128)(2,1)S(1)}, bf16[512,192]{1,0:T(8,128)(2,1)S(1)}, bf16[128,4096]{1,0:T(8,128)(2,1)S(1)}) custom-call(bf16[1,8,4096]{2,1,0:T(8,128)(2,1)} %refs_0_.1, bf16[1,8,4096]{2,1,0:T(8,128)(2,1)} %refs_1_.1, s32[8,64]{1,0:T(8,128)} %bitcast.14, bf16[8,64]{1,0:T(8,128)(2,1)} %bitcast.15, ...), custom_call_target="tpu_custom_call" | custom-call | tf_op jit(solution)/shard_map/first/pallas_call | solution.py:282
  2.3 0.0 copy-start.1
  2.3 13.3 %all_to_all.20 = bf16[8,2,8,1024]{3,2,1,0:T(8,128)(2,1)S(1)} all-to-all(bf16[8,2,8,1024]{3,2,1,0:T(8,128)(2,1)S(1)} %get-tuple-element.10), channel_id=1, replica_groups={{512,0,640,128,384,896,256,768},{513,1,641,129,385,897,257,769},{514,2,..., dimensions={0} | all-to-all | bytes 524288 | tf_op jit(solution)/shard_map/all_to_all | solution.py:21
  15.6 0.0 copy-start
  15.6 0.3 pack.1
  15.9 24.3 %all_to_all.21.refs_0_ = bf16[16,48,256]{2,1,0:T(8,128)(2,1)S(1)} all-to-all(bf16[16,48,256]{2,1,0:T(8,128)(2,1)S(1)} %pack.1), channel_id=1, replica_groups={{4,64,228,160,100,32,196,128,68,0,164,224,36,96,132,192},{5,65,229,161,..., dimensions={0} | all-to-all | bytes 786432 | tf_op jit(solution)/shard_map/all_to_all | solution.py:21
  40.2 0.0 copy-done.1
  40.2 0.0 copy-done
  40.2 1.8 %expert.1 = bf16[32,48,128]{2,1,0:T(8,128)(2,1)S(1)} custom-call(bf16[16,48,256]{2,1,0:T(8,128)(2,1)S(1)} %all_to_all.21.refs_0_, bf16[4096,128]{1,0:T(8,128)(2,1)S(1)} %bitcast.12, bf16[4096,128]{1,0:T(8,128)(2,1)S(1)} %bitcast.13, bf16[128,4096]{1,0:T(8,128)(2,1)S(1)} %get-tuple-element.11.refs_3_), custom_call_target="tpu_custom_call" | custom-call | tf_op jit(solution)/shard_map/expert/pallas_call | solution.py:314
  42.0 17.3 %all_to_all.22.refs_1_ = bf16[32,48,128]{2,1,0:T(8,128)(2,1)S(1)} all-to-all(bf16[32,48,128]{2,1,0:T(8,128)(2,1)S(1)} %expert.1), channel_id=1, replica_groups={{512,224,832,416,0,736,320,928,544,128,864,448,32,640,352,960,576,160,7..., dimensions={0} | all-to-all | bytes 786432 | tf_op jit(solution)/shard_map/all_to_all | solution.py:21
  59.2 0.2 combine.1
  59.5 20.4 %all_to_all.23.got_ref = bf16[32,16,128]{2,1,0:T(8,128)(2,1)S(1)} all-to-all(bf16[32,16,128]{2,1,0:T(8,128)(2,1)S(1)} %combine.1), channel_id=1, replica_groups={{30,17,4,27,14,1,20,11,31,18,5,24,15,2,21,8,28,19,6,25,12,3,22,9,29,16,..., dimensions={0} | all-to-all | bytes 262144 | tf_op jit(solution)/shard_map/all_to_all | solution.py:21
  79.8 0.6 finish.1
Async XLA Ops:
  2.3 37.9 %copy-start.1 = (bf16[1,4096,128]{2,1,0:T(8,128)(2,1)S(1)}, bf16[1,4096,128]{2,1,0:T(8,128)(2,1)}, u32[]{:S(2)}) copy-start(bf16[1,4096,128]{2,1,0:T(8,128)(2,1)} %param.12) | copy-start | bytes 3145732
  15.6 24.6 %copy-start = (bf16[1,4096,128]{2,1,0:T(8,128)(2,1)S(1)}, bf16[1,4096,128]{2,1,0:T(8,128)(2,1)}, u32[]{:S(2)}) copy-start(bf16[1,4096,128]{2,1,0:T(8,128)(2,1)} %param.11) | copy-start | bytes 3145732

commit v7 on v6

--- a/solution.py
+++ b/solution.py
@@ -259,9 +259,8 @@
     tp_count = lax.axis_size("za") * lax.axis_size("zb") * lax.axis_size("xh")
     _, own_rows, width = tokens.shape
     column, top = routes.shape[1:]
-    dp_order = [(4 + step) % dp_count for step in (0, 4, 1, 5, 7, 3, 6, 2)]
     orders = (
-        dp_order,
+        [(4 + 3 * j) % dp_count for j in range(dp_count)],
         [(1 + 7 * j) % (ctx_count * 4) for j in range(ctx_count * 4)],
         [
             (j // dp_count + 3 * j) % ctx_count * dp_count + (4 + 5 * j) % dp_count

time: 80.7 us -> 79.5 us (0.985)
  blocking collectives: 75.2 us -> 73.7 us
    all_to_all x4, blocking collectives: 75.2 us -> 73.7 us  [exchange(): lax.all_to_all(v, axes, split_axis=0, concat_axis=0, axis_index_groups=[o...]
where the time goes in v7:
time: 79.5 us; the launch traced here: 78.9 us
  blocking collectives  73.7 us (93%)
  Pallas kernels  4.58 us (6%)
    all_to_all x4, blocking collectives, exchange(): lax.all_to_all(v, axes, split_axis=0, concat_axis=0, axis_index_groups=[o...  73.7 us
    pallas_call x1, Pallas kernels, body(): pl.pallas_call(lambda *refs: expert_kernel(ctx_count, orders[1], orders[2...  1.8 us
    pallas_call x1, Pallas kernels, body(): pl.pallas_call(lambda *refs: first_kernel(ctx_count, tp_count, orders[0],...  1.66 us

profile of v7, /device:TPU:1, one launch (start us, length us, event | category | flops | bytes accessed | tf_op | source)
XLA Modules:
  0.0 78.9 jit_solution(1696315662454842971)
XLA Ops:
  0.6 1.7 %first.1 = (bf16[8,2,8,1024]{3,2,1,0:T(8,128)(2,1)S(1)}, bf16[384,512]{1,0:T(8,128)(2,1)S(1)}, bf16[512,192]{1,0:T(8,128)(2,1)S(1)}, bf16[128,4096]{1,0:T(8,128)(2,1)S(1)}) custom-call(bf16[1,8,4096]{2,1,0:T(8,128)(2,1)} %refs_0_.1, bf16[1,8,4096]{2,1,0:T(8,128)(2,1)} %refs_1_.1, s32[8,64]{1,0:T(8,128)} %bitcast.14, bf16[8,64]{1,0:T(8,128)(2,1)} %bitcast.15, ...), custom_call_target="tpu_custom_call" | custom-call | tf_op jit(solution)/shard_map/first/pallas_call | solution.py:281
  2.3 0.0 copy-start.1
  2.3 13.3 %all_to_all.20 = bf16[8,2,8,1024]{3,2,1,0:T(8,128)(2,1)S(1)} all-to-all(bf16[8,2,8,1024]{3,2,1,0:T(8,128)(2,1)S(1)} %get-tuple-element.10), channel_id=1, replica_groups={{512,896,256,640,0,384,768,128},{513,897,257,641,1,385,769,129},{514,89..., dimensions={0} | all-to-all | bytes 524288 | tf_op jit(solution)/shard_map/all_to_all | solution.py:21
  15.6 0.0 copy-start
  15.6 0.3 pack.1
  15.9 24.0 %all_to_all.21.refs_0_ = bf16[16,48,256]{2,1,0:T(8,128)(2,1)S(1)} all-to-all(bf16[16,48,256]{2,1,0:T(8,128)(2,1)S(1)} %pack.1), channel_id=1, replica_groups={{4,64,228,160,100,32,196,128,68,0,164,224,36,96,132,192},{5,65,229,161,..., dimensions={0} | all-to-all | bytes 786432 | tf_op jit(solution)/shard_map/all_to_all | solution.py:21
  39.8 0.0 copy-done.1
  39.8 0.0 copy-done
  39.8 1.8 %expert.1 = bf16[32,48,128]{2,1,0:T(8,128)(2,1)S(1)} custom-call(bf16[16,48,256]{2,1,0:T(8,128)(2,1)S(1)} %all_to_all.21.refs_0_, bf16[4096,128]{1,0:T(8,128)(2,1)S(1)} %bitcast.12, bf16[4096,128]{1,0:T(8,128)(2,1)S(1)} %bitcast.13, bf16[128,4096]{1,0:T(8,128)(2,1)S(1)} %get-tuple-element.11.refs_3_), custom_call_target="tpu_custom_call" | custom-call | tf_op jit(solution)/shard_map/expert/pallas_call | solution.py:313
  41.6 17.3 %all_to_all.22.refs_1_ = bf16[32,48,128]{2,1,0:T(8,128)(2,1)S(1)} all-to-all(bf16[32,48,128]{2,1,0:T(8,128)(2,1)S(1)} %expert.1), channel_id=1, replica_groups={{512,224,832,416,0,736,320,928,544,128,864,448,32,640,352,960,576,160,7..., dimensions={0} | all-to-all | bytes 786432 | tf_op jit(solution)/shard_map/all_to_all | solution.py:21
  58.9 0.2 combine.1
  59.1 19.2 %all_to_all.23.got_ref = bf16[32,16,128]{2,1,0:T(8,128)(2,1)S(1)} all-to-all(bf16[32,16,128]{2,1,0:T(8,128)(2,1)S(1)} %combine.1), channel_id=1, replica_groups={{30,17,4,27,14,1,20,11,31,18,5,24,15,2,21,8,28,19,6,25,12,3,22,9,29,16,..., dimensions={0} | all-to-all | bytes 262144 | tf_op jit(solution)/shard_map/all_to_all | solution.py:21
  78.3 0.6 finish.1
Async XLA Ops:
  2.3 37.5 %copy-start.1 = (bf16[1,4096,128]{2,1,0:T(8,128)(2,1)S(1)}, bf16[1,4096,128]{2,1,0:T(8,128)(2,1)}, u32[]{:S(2)}) copy-start(bf16[1,4096,128]{2,1,0:T(8,128)(2,1)} %param.12) | copy-start | bytes 3145732
  15.6 24.3 %copy-start = (bf16[1,4096,128]{2,1,0:T(8,128)(2,1)S(1)}, bf16[1,4096,128]{2,1,0:T(8,128)(2,1)}, u32[]{:S(2)}) copy-start(bf16[1,4096,128]{2,1,0:T(8,128)(2,1)} %param.11) | copy-start | bytes 3145732

commit v8 on v7

--- a/solution.py
+++ b/solution.py
@@ -66,8 +66,9 @@
 
     shape = (column, columns)
     spread = (iota(shape, 0) == token(iota(shape, 1))).astype(F32).astype(BF16)
-    routes = dot(routes_ref[...].astype(F32).astype(BF16), spread)
-    probs = dot(probs_ref[...], spread)
+    both = jnp.concatenate((routes_ref[...].astype(F32), probs_ref[...].astype(F32)), axis=0)
+    both = dot(both.astype(BF16), spread)
+    routes, probs = both[:top], both[top:]
     for k in range(top):
         hit = routes[k : k + 1, :] == expert
         named = jnp.where(hit, 1.0, named)
@@ -79,34 +80,30 @@
     before = dot(named, earlier)
     table = jnp.concatenate((named, share.astype(BF16), before.astype(BF16)), axis=1)
 
-    def picked(expert_rows, slot_rows):
-        wanted = (expert_rows == iota(expert_rows.shape, 1)).astype(F32).astype(BF16)
-        got = dot(wanted, table)
-        valid = (got[:, :columns] > 0.5) & (
-            got[:, 2 * columns :] == slot_rows.astype(F32)
-        )
-        return valid, got[:, columns : 2 * columns]
-
-    row = iota((ctx_count * 2 * CUTS * 2 * CAP, LANES), 0)
-    outer = sixth(row)
-    slot = row - CAP * outer
-    kind = outer & 1
-    cut = (outer >> 1) & 3
-    far = outer >> 3
+    def parts(rows):
+        row = iota((rows, LANES), 0)
+        outer = sixth(row)
+        return row - CAP * outer, outer & 1, (outer >> 1) & 3, outer >> 3
+
+    slot, kind, cut, far = parts(ctx_count * 2 * CUTS * 2 * CAP)
     owner = (far >> 1) * tp_count + (za * 2 + (far & 1)) * X_PARTS + xh
-    valid, scale = picked(owner, slot)
-    mine = valid & (kind == kind_of(iota(row.shape, 1)))
-    value = jnp.where(mine, jnp.where(kind == 1, scale, 1.0), 0.0)
+    own_slot, own_kind, _, own_far = parts(ctx_count * CUTS * 2 * CAP)
+    own_owner = own_far * tp_count + (za * 2 + zb) * X_PARTS + xh
+    owners = jnp.concatenate((owner, own_owner), axis=0)
+    slots = jnp.concatenate((slot, own_slot), axis=0).astype(F32)
+    got = dot((owners == iota(owners.shape, 1)).astype(F32).astype(BF16), table)
+    valid = (got[:, :columns] > 0.5) & (got[:, 2 * columns :] == slots)
+    scale = got[:, columns : 2 * columns]
+    count = slot.shape[0]
+
+    mine = valid[:count] & (kind == kind_of(iota(slot.shape, 1)))
+    value = jnp.where(mine, jnp.where(kind == 1, scale[:count], 1.0), 0.0)
     for c in range(CUTS):
         pack_ref[:, c * LANES : (c + 1) * LANES] = jnp.where(cut == c, value, 0.0).astype(BF16)
 
-    row = iota((ctx_count * CUTS * 2 * CAP, LANES), 0)
-    outer = sixth(row)
-    slot = row - CAP * outer
-    kind = outer & 1
-    owner = (outer >> 3) * tp_count + (za * 2 + zb) * X_PARTS + xh
-    valid, scale = picked(owner, slot)
-    value = jnp.where(valid, jnp.where(kind == 0, scale, 1.0), 0.0).astype(BF16)
+    value = jnp.where(
+        valid[count:], jnp.where(own_kind == 0, scale[count:], 1.0), 0.0
+    ).astype(BF16)
     shape = (mix_ref.shape[0], LANES)
     row, col = iota(shape, 0), iota(shape, 1)
     wanted = (kind_of(col) == 0) & (token(col) == ((row >> 4) << 1) + (row & 1))
@@ -260,7 +257,7 @@
     _, own_rows, width = tokens.shape
     column, top = routes.shape[1:]
     orders = (
-        [(4 + 3 * j) % dp_count for j in range(dp_count)],
+        [(5 + 3 * j) % dp_count for j in range(dp_count)],
         [(1 + 7 * j) % (ctx_count * 4) for j in range(ctx_count * 4)],
         [
             (j // dp_count + 3 * j) % ctx_count * dp_count + (4 + 5 * j) % dp_count

time: 79.5 us -> 79.7 us (level)
  no operation moved by 1% of the time
where the time goes in v8:
time: 79.7 us; the launch traced here: 79.1 us
  blocking collectives  73.8 us (93%)
  Pallas kernels  4.56 us (6%)
    all_to_all x4, blocking collectives, exchange(): lax.all_to_all(v, axes, split_axis=0, concat_axis=0, axis_index_groups=[o...  73.8 us
    pallas_call x1, Pallas kernels, body(): pl.pallas_call(lambda *refs: expert_kernel(ctx_count, orders[1], orders[2...  1.8 us
    pallas_call x1, Pallas kernels, body(): pl.pallas_call(lambda *refs: first_kernel(ctx_count, tp_count, orders[0],...  1.65 us

profile of v8, /device:TPU:1, one launch (start us, length us, event | category | flops | bytes accessed | tf_op | source)
XLA Modules:
  0.0 79.1 jit_solution(11716229441331359563)
XLA Ops:
  0.6 1.6 %first.1 = (bf16[8,2,8,1024]{3,2,1,0:T(8,128)(2,1)S(1)}, bf16[384,512]{1,0:T(8,128)(2,1)S(1)}, bf16[512,192]{1,0:T(8,128)(2,1)S(1)}, bf16[128,4096]{1,0:T(8,128)(2,1)S(1)}) custom-call(bf16[1,8,4096]{2,1,0:T(8,128)(2,1)} %refs_0_.1, bf16[1,8,4096]{2,1,0:T(8,128)(2,1)} %refs_1_.1, s32[8,64]{1,0:T(8,128)} %bitcast.14, bf16[8,64]{1,0:T(8,128)(2,1)} %bitcast.15, ...), custom_call_target="tpu_custom_call" | custom-call | tf_op jit(solution)/shard_map/first/pallas_call | solution.py:278
  2.3 0.0 copy-start.1
  2.3 13.1 %all_to_all.20 = bf16[8,2,8,1024]{3,2,1,0:T(8,128)(2,1)S(1)} all-to-all(bf16[8,2,8,1024]{3,2,1,0:T(8,128)(2,1)S(1)} %get-tuple-element.10), channel_id=1, replica_groups={{640,0,384,768,128,512,896,256},{641,1,385,769,129,513,897,257},{642,2,..., dimensions={0} | all-to-all | bytes 524288 | tf_op jit(solution)/shard_map/all_to_all | solution.py:21
  15.4 0.0 copy-start
  15.4 0.3 pack.1
  15.7 23.6 %all_to_all.21.refs_0_ = bf16[16,48,256]{2,1,0:T(8,128)(2,1)S(1)} all-to-all(bf16[16,48,256]{2,1,0:T(8,128)(2,1)S(1)} %pack.1), channel_id=1, replica_groups={{4,64,228,160,100,32,196,128,68,0,164,224,36,96,132,192},{5,65,229,161,..., dimensions={0} | all-to-all | bytes 786432 | tf_op jit(solution)/shard_map/all_to_all | solution.py:21
  39.3 0.0 copy-done.1
  39.3 0.0 copy-done
  39.3 1.8 %expert.1 = bf16[32,48,128]{2,1,0:T(8,128)(2,1)S(1)} custom-call(bf16[16,48,256]{2,1,0:T(8,128)(2,1)S(1)} %all_to_all.21.refs_0_, bf16[4096,128]{1,0:T(8,128)(2,1)S(1)} %bitcast.12, bf16[4096,128]{1,0:T(8,128)(2,1)S(1)} %bitcast.13, bf16[128,4096]{1,0:T(8,128)(2,1)S(1)} %get-tuple-element.11.refs_3_), custom_call_target="tpu_custom_call" | custom-call | tf_op jit(solution)/shard_map/expert/pallas_call | solution.py:310
  41.1 17.7 %all_to_all.22.refs_1_ = bf16[32,48,128]{2,1,0:T(8,128)(2,1)S(1)} all-to-all(bf16[32,48,128]{2,1,0:T(8,128)(2,1)S(1)} %expert.1), channel_id=1, replica_groups={{512,224,832,416,0,736,320,928,544,128,864,448,32,640,352,960,576,160,7..., dimensions={0} | all-to-all | bytes 786432 | tf_op jit(solution)/shard_map/all_to_all | solution.py:21
  58.7 0.2 combine.1
  59.0 19.5 %all_to_all.23.got_ref = bf16[32,16,128]{2,1,0:T(8,128)(2,1)S(1)} all-to-all(bf16[32,16,128]{2,1,0:T(8,128)(2,1)S(1)} %combine.1), channel_id=1, replica_groups={{30,17,4,27,14,1,20,11,31,18,5,24,15,2,21,8,28,19,6,25,12,3,22,9,29,16,..., dimensions={0} | all-to-all | bytes 262144 | tf_op jit(solution)/shard_map/all_to_all | solution.py:21
  78.4 0.6 finish.1
Async XLA Ops:
  2.3 37.0 %copy-start.1 = (bf16[1,4096,128]{2,1,0:T(8,128)(2,1)S(1)}, bf16[1,4096,128]{2,1,0:T(8,128)(2,1)}, u32[]{:S(2)}) copy-start(bf16[1,4096,128]{2,1,0:T(8,128)(2,1)} %param.12) | copy-start | bytes 3145732
  15.4 23.8 %copy-start = (bf16[1,4096,128]{2,1,0:T(8,128)(2,1)S(1)}, bf16[1,4096,128]{2,1,0:T(8,128)(2,1)}, u32[]{:S(2)}) copy-start(bf16[1,4096,128]{2,1,0:T(8,128)(2,1)} %param.11) | copy-start | bytes 3145732
